TPU v7x, 512 devices: a whole 4x4x16 slice. The times are simulated.
512 devices in a mesh: seq: 256 (over z, y, x_hi, core), head: 2 (over x_lo).
Axes of the slice: x: 4 (x_hi: 2, x_lo: 2; x = x_hi * 2 + x_lo), y: 4, z: 16, core: 2. Of those that a mesh axis runs over, the one named last changes fastest.
Arguments:
- queries: bfloat16 [2, 262144, 128], P('head', 'seq'), may hold values from -88 to 88
- keys: bfloat16 [2, 262144, 128], P('head', 'seq'), may hold values from -4 to 4
- values: bfloat16 [2, 262144, 128], P('head', 'seq'), may hold values from -5 to 5
- out_grad: bfloat16 [2, 262144, 128], P('head', 'seq'), may hold values from -5 to 5
- route: int32 [2, 256], P('head', 'seq'), may hold values from 0 to 255, as said below
Outputs:
- attended: bfloat16 [2, 262144, 128], P('head', 'seq')
- query_grad: bfloat16 [2, 262144, 128], P('head', 'seq')
- key_grad: bfloat16 [2, 262144, 128], P('head', 'seq')
- value_grad: bfloat16 [2, 262144, 128], P('head', 'seq')
Inputs may be any that keep to these rules, and one draw needn't show every extreme that they name: Bit s of route[h, j] equals bit s of route[h, j XOR 2^s], so partner is a permutation of the blocks for each head.
All inputs are finite; a program needn't handle non-finite values.
Results may differ from a plain program's by a relative error of at most 0.029.
Values may be sent and summed in bfloat16 or wider, within the bound.
No kernel may reach another device: no remote copies, remote signals or barrier semaphores. Data moves between devices by JAX's collectives and lax.ppermute only.
A program may use at most 64 MiB of HBM per device.

v0:
```python
import jax
import jax.numpy as jnp
from jax import lax
from jax.sharding import PartitionSpec as P


def from_behind(block, axis, distance):
    devices = range(lax.axis_size(axis))
    route = [(i - distance, i) for i in devices if i - distance in devices]
    return lax.ppermute(block, axis, route)


def from_partner(x, axis, stride):
    return lax.ppermute(x, axis, [(i, i ^ 1 << stride) for i in range(lax.axis_size(axis))])


def allowed_cols(offset, count, rows_dev, leading):
    qpos = offset + jnp.arange(count)[:, None]
    kidx = jnp.arange(3 * rows_dev)[None, :]
    own_part = (kidx < rows_dev) & (kidx <= qpos)
    prev_part = (kidx >= rows_dev) & (kidx < 2 * rows_dev) & jnp.logical_not(leading)
    return own_part | prev_part | (kidx >= 2 * rows_dev)


def local(queries, keys, values, out_grad, route):
    query_rows = queries[0]
    key_rows = keys[0]
    value_rows = values[0]
    grad_rows = out_grad[0]
    rows_dev, head_width = query_rows.shape
    factor = head_width ** (-0.5)
    levels = lax.axis_size("seq").bit_length() - 1
    switches = route[0, 0]
    leading = lax.axis_index("seq") == 0
    columns = 3 * rows_dev
    key_before, value_before = from_behind((key_rows, value_rows), "seq", 1)
    key_partner, value_partner = (key_rows, value_rows)
    for level in range(levels):
        other_key, other_value = from_partner((key_partner, value_partner), "seq", level)
        taken = switches // 2**level % 2 == 1
        key_partner = jnp.where(taken, other_key, key_partner)
        value_partner = jnp.where(taken, other_value, value_partner)
    keys_all = jnp.concatenate([key_rows, key_before, key_partner], 0)
    values_all = jnp.concatenate([value_rows, value_before, value_partner], 0)
    block_rows = min(512, rows_dev)
    count = rows_dev // block_rows
    offsets = jnp.arange(count, dtype=jnp.int32) * block_rows
    query_blocks = query_rows.reshape(count, block_rows, head_width)
    grad_blocks = grad_rows.reshape(count, block_rows, head_width)

    def forward_rows(packed):
        block, offset = packed
        scores = (
            jnp.einsum("qd,kd->qk", block, keys_all, preferred_element_type=jnp.float32) * factor
        )
        scores = jnp.where(allowed_cols(offset, block_rows, rows_dev, leading), scores, -jnp.inf)
        peak = jnp.max(scores, -1, keepdims=True)
        log_total = peak[:, 0] + jnp.log(jnp.sum(jnp.exp(scores - peak), -1))
        weights_bf = jnp.exp(scores - log_total[:, None]).astype(jnp.bfloat16)
        attended = jnp.einsum(
            "qk,kd->qd", weights_bf, values_all, preferred_element_type=jnp.float32
        ).astype(jnp.bfloat16)
        return (attended, weights_bf, log_total)

    attended_blocks, weight_blocks, total_blocks = lax.map(forward_rows, (query_blocks, offsets))
    attended = attended_blocks.reshape(rows_dev, head_width)
    correction = jnp.sum(grad_rows.astype(jnp.float32) * attended.astype(jnp.float32), -1)
    drift_blocks = correction.reshape(count, block_rows)

    def backward_rows(carry, packed):
        key_acc, value_acc = carry
        block, grad_block, weights_bf, drift = packed
        pushed = jnp.einsum("qd,kd->qk", grad_block, values_all, preferred_element_type=jnp.float32)
        shaped = (weights_bf.astype(jnp.float32) * (pushed - drift[:, None])).astype(jnp.bfloat16)
        query_part = (
            jnp.einsum("qk,kd->qd", shaped, keys_all, preferred_element_type=jnp.float32) * factor
        ).astype(jnp.bfloat16)
        key_acc = (
            key_acc
            + jnp.einsum("qk,qd->kd", shaped, block, preferred_element_type=jnp.float32) * factor
        )
        value_acc = value_acc + jnp.einsum(
            "qk,qd->kd", weights_bf, grad_block, preferred_element_type=jnp.float32
        )
        return ((key_acc, value_acc), query_part)

    empty = jnp.zeros((columns, head_width), jnp.float32)
    (key_acc, value_acc), query_parts = lax.scan(
        backward_rows, (empty, empty), (query_blocks, grad_blocks, weight_blocks, drift_blocks)
    )
    query_grad = query_parts.reshape(rows_dev, head_width)
    key_back, value_back = from_behind(
        (
            key_acc[rows_dev : 2 * rows_dev].astype(jnp.bfloat16),
            value_acc[rows_dev : 2 * rows_dev].astype(jnp.bfloat16),
        ),
        "seq",
        -1,
    )
    partner_key = key_acc[2 * rows_dev :].astype(jnp.bfloat16)
    partner_value = value_acc[2 * rows_dev :].astype(jnp.bfloat16)
    for level in reversed(range(levels)):
        other_key, other_value = from_partner((partner_key, partner_value), "seq", level)
        taken = switches // 2**level % 2 == 1
        partner_key = jnp.where(taken, other_key, partner_key)
        partner_value = jnp.where(taken, other_value, partner_value)
    key_grad = (
        key_acc[:rows_dev] + key_back.astype(jnp.float32) + partner_key.astype(jnp.float32)
    ).astype(jnp.bfloat16)
    value_grad = (
        value_acc[:rows_dev] + value_back.astype(jnp.float32) + partner_value.astype(jnp.float32)
    ).astype(jnp.bfloat16)
    return (attended[None], query_grad[None], key_grad[None], value_grad[None])


def solution(mesh):
    return jax.shard_map(
        local,
        mesh=mesh,
        in_specs=(
            P("head", "seq", None),
            P("head", "seq", None),
            P("head", "seq", None),
            P("head", "seq", None),
            P("head", "seq"),
        ),
        out_specs=(
            P("head", "seq", None),
            P("head", "seq", None),
            P("head", "seq", None),
            P("head", "seq", None),
        ),
        check_vma=False,
    )
```

profile of v0, /device:TPU:1, one launch (start us, length us, event | category | flops | bytes accessed | tf_op | source)
XLA Modules:
  0.0 383.9 jit_solution(5414099422173744608)
XLA Ops:
  0.6 8.8 %collective-permute-start.10 = (bf16[1024,128]{1,0:T(8,128)(2,1)}, bf16[1024,128]{1,0:T(8,128)(2,1)S(1)}, u32[]{:S(2)}, u32[]{:S(2)}) collective-permute-start(bf16[1024,128]{1,0:T(8,128)(2,1)} %bitcast.94), channel_id=1, source_target_pairs={{0,2},{2,0},{4,6},{6,4},{8,10},{10,8},{12,14},{14,12},{16,18},{18,... | collective-permute-start | bytes 786440 | tf_op jit(solution)/shard_map/ppermute | solution.py:14
  9.4 1.9 collective-permute-start.1
  13.0 1.9 collective-permute-start.11
  16.0 4.9 %collective-permute-start.2 = (bf16[1024,128]{1,0:T(8,128)(2,1)S(1)}, bf16[1024,128]{1,0:T(8,128)(2,1)S(1)}, u32[]{:S(2)}, u32[]{:S(2)}) collective-permute-start(bf16[1024,128]{1,0:T(8,128)(2,1)S(1)} %broadcast_select_fusion.1), channel_id=1, source_target_pairs={{0,4},{2,6},{4,0},{6,2},{8,12},{10,14},{12,8},{14,10},{16,20},{18,... | collective-permute-start | bytes 786440 | tf_op jit(solution)/shard_map/ppermute | solution.py:14
  20.9 2.9 collective-permute-done.11
  23.8 1.9 collective-permute-start.12
  25.8 3.6 collective-permute-done.2
  29.4 1.9 collective-permute-start.3
  31.4 1.9 collective-permute-start.13
  33.4 4.4 %collective-permute-done.3 = bf16[1024,128]{1,0:T(8,128)(2,1)S(1)} collective-permute-done((bf16[1024,128]{1,0:T(8,128)(2,1)S(1)}, bf16[1024,128]{1,0:T(8,128)(2,1)S(1)}, u32[]{:S(2)}, u32[]{:S(2)}) %collective-permute-start.3) | collective-permute-done | bytes 262176 | tf_op jit(solution)/shard_map/ppermute | solution.py:14
  37.8 1.9 collective-permute-start.4
  41.5 2.4 collective-permute-start.14
  44.0 3.1 collective-permute-done.4
  47.1 2.4 collective-permute-start.5
  49.6 4.9 %collective-permute-start.15 = (bf16[1024,128]{1,0:T(8,128)(2,1)S(1)}, bf16[1024,128]{1,0:T(8,128)(2,1)S(1)}, u32[]{:S(2)}, u32[]{:S(2)}) collective-permute-start(bf16[1024,128]{1,0:T(8,128)(2,1)S(1)} %broadcast_select_fusion.16), channel_id=1, source_target_pairs={{0,64},{2,66},{4,68},{6,70},{8,72},{10,74},{12,76},{14,78},{16,80}... | collective-permute-start | bytes 786440 | tf_op jit(solution)/shard_map/ppermute | solution.py:14
  55.5 7.9 %collective-permute-start.6 = (bf16[1024,128]{1,0:T(8,128)(2,1)S(1)}, bf16[1024,128]{1,0:T(8,128)(2,1)S(1)}, u32[]{:S(2)}, u32[]{:S(2)}) collective-permute-start(bf16[1024,128]{1,0:T(8,128)(2,1)S(1)} %broadcast_select_fusion.17), channel_id=1, source_target_pairs={{0,64},{2,66},{4,68},{6,70},{8,72},{10,74},{12,76},{14,78},{16,80}... | collective-permute-start | bytes 786440 | tf_op jit(solution)/shard_map/ppermute | solution.py:14
  63.5 8.8 %collective-permute-start.16 = (bf16[1024,128]{1,0:T(8,128)(2,1)S(1)}, bf16[1024,128]{1,0:T(8,128)(2,1)S(1)}, u32[]{:S(2)}, u32[]{:S(2)}) collective-permute-start(bf16[1024,128]{1,0:T(8,128)(2,1)S(1)} %broadcast_select_fusion.20), channel_id=1, source_target_pairs={{0,128},{2,130},{4,132},{6,134},{8,136},{10,138},{12,140},{14,142}... | collective-permute-start | bytes 786440 | tf_op jit(solution)/shard_map/ppermute | solution.py:14
  72.3 21.0 %collective-permute-start.9 = (bf16[1024,128]{1,0:T(8,128)(2,1)S(1)}, bf16[1024,128]{1,0:T(8,128)(2,1)S(1)}, u32[]{:S(2)}, u32[]{:S(2)}) collective-permute-start(bf16[1024,128]{1,0:T(8,128)(2,1)S(1)} %bitcast.95), channel_id=1, source_target_pairs={{0,2},{2,4},{4,6},{6,8},{8,10},{10,12},{12,14},{14,16},{16,18},{18... | collective-permute-start | bytes 786440 | tf_op jit(solution)/shard_map/ppermute | solution.py:10
  93.3 1.9 collective-permute-start
  95.3 3.3 collective-permute-start.7
  98.7 12.7 %collective-permute-start.17 = (bf16[1024,128]{1,0:T(8,128)(2,1)S(1)}, bf16[1024,128]{1,0:T(8,128)(2,1)S(1)}, u32[]{:S(2)}, u32[]{:S(2)}) collective-permute-start(bf16[1024,128]{1,0:T(8,128)(2,1)S(1)} %broadcast_select_fusion.24), channel_id=1, source_target_pairs={{0,256},{2,258},{4,260},{6,262},{8,264},{10,266},{12,268},{14,270}... | collective-permute-start | bytes 786440 | tf_op jit(solution)/shard_map/ppermute | solution.py:14
  111.5 36.5 %collective-permute-done.7 = bf16[1024,128]{1,0:T(8,128)(2,1)S(1)} collective-permute-done((bf16[1024,128]{1,0:T(8,128)(2,1)S(1)}, bf16[1024,128]{1,0:T(8,128)(2,1)S(1)}, u32[]{:S(2)}, u32[]{:S(2)}) %collective-permute-start.7) | collective-permute-done | bytes 262176 | tf_op jit(solution)/shard_map/ppermute | solution.py:14
  148.0 10.0 %collective-permute-start.8 = (bf16[1024,128]{1,0:T(8,128)(2,1)S(1)}, bf16[1024,128]{1,0:T(8,128)(2,1)S(1)}, u32[]{:S(2)}, u32[]{:S(2)}) collective-permute-start(bf16[1024,128]{1,0:T(8,128)(2,1)S(1)} %broadcast_select_fusion.25), channel_id=1, source_target_pairs={{0,256},{2,258},{4,260},{6,262},{8,264},{10,266},{12,268},{14,270}... | collective-permute-start | bytes 786440 | tf_op jit(solution)/shard_map/ppermute | solution.py:14
  158.2 9.5 %collective-permute-done.8 = bf16[1024,128]{1,0:T(8,128)(2,1)S(1)} collective-permute-done((bf16[1024,128]{1,0:T(8,128)(2,1)S(1)}, bf16[1024,128]{1,0:T(8,128)(2,1)S(1)}, u32[]{:S(2)}, u32[]{:S(2)}) %collective-permute-start.8) | collective-permute-done | bytes 262176 | tf_op jit(solution)/shard_map/ppermute | solution.py:14
  167.9 19.1 %while.29 = (s32[]{:T(128)}, bf16[2,512,128]{2,1,0:T(8,128)(2,1)S(1)}, bf16[2,512,3072]{2,1,0:T(8,128)(2,1)}, s32[2]{0:T(128)S(1)}, pred[]{:T(512)}, /*index=5*/...) while((s32[]{:T(128)}, ...), condition=%wide.region_3.4_spmd, body=%wide.region_0.3_spmd.sunk | while | flops 825837568 | bytes 30186608 | solution.py:65
  169.2 3.3 fusion.53
  173.5 2.8 bitcast_dynamic-update-slice_fusion.2
  178.7 3.3 fusion.53
  183.0 2.9 bitcast_dynamic-update-slice_fusion.2
  188.0 30.1 %while.30 = (s32[]{:T(128)}, f32[3072,128]{1,0:T(8,128)}, f32[3072,128]{1,0:T(8,128)}, bf16[2,512,128]{2,1,0:T(8,128)(2,1)}, bf16[2,512,3072]{2,1,0:T(8,128)(2,1...) while((s32[]{:T(128)}, f32[3072,128]{1,0:T(8,128)}, ...), condition=%wide.region_6.7_spmd.clone, body=%wide.region_5.6_spmd.clone.sunk | while | flops 1619001344 | bytes 38806320 | solution.py:88
  189.2 3.1 multiply_convert_fusion.2
  192.3 3.1 fusion.63
  195.5 2.2 fusion.64
  198.3 4.2 %convolution_add_fusion.2 = f32[3072,128]{1,0:T(8,128)} fusion(bf16[2,512,3072]{2,1,0:T(8,128)(2,1)} %get-tuple-element.408, s32[]{:T(128)} %get-tuple-element.392, f32[3072,128]{1,0:T(8,128)} %get-tuple-element.394, pred[]{:T(512)S(6)} %compare.26, bf16[2,512,128]{2,1,0:T(8,128)(2,1)S(1)} %get-tuple-element.409), kind=kOutput, calls=%fused_computation.23.clone.1 | convolution fusion | flops 403439616 | bytes 6423553 | tf_op jit(solution)/shard_map/while/body/eval_jaxpr/qk,qd->kd/dot_general | solution.py:82
  203.7 3.1 multiply_convert_fusion.2
  206.9 3.7 fusion.63
  210.6 2.2 fusion.64
  213.5 4.7 %convolution_add_fusion.2 = f32[3072,128]{1,0:T(8,128)} fusion(bf16[2,512,3072]{2,1,0:T(8,128)(2,1)} %get-tuple-element.408, s32[]{:T(128)} %get-tuple-element.392, f32[3072,128]{1,0:T(8,128)} %get-tuple-element.394, pred[]{:T(512)S(6)} %compare.26, bf16[2,512,128]{2,1,0:T(8,128)(2,1)S(1)} %get-tuple-element.409), kind=kOutput, calls=%fused_computation.23.clone.1 | convolution fusion | flops 403439616 | bytes 6423553 | tf_op jit(solution)/shard_map/while/body/eval_jaxpr/qk,qd->kd/dot_general | solution.py:82
  219.8 12.2 %collective-permute-start.28 = (bf16[1024,128]{1,0:T(8,128)(2,1)S(1)}, bf16[1024,128]{1,0:T(8,128)(2,1)S(1)}, u32[]{:S(2)}, u32[]{:S(2)}) collective-permute-start(bf16[1024,128]{1,0:T(8,128)(2,1)S(1)} %slice.31), channel_id=1, source_target_pairs={{0,256},{2,258},{4,260},{6,262},{8,264},{10,266},{12,268},{14,270}... | collective-permute-start | bytes 786440 | tf_op jit(solution)/shard_map/ppermute | solution.py:14
  232.1 1.9 collective-permute-start.19
  234.0 10.2 %collective-permute-done.28 = bf16[1024,128]{1,0:T(8,128)(2,1)S(1)} collective-permute-done((bf16[1024,128]{1,0:T(8,128)(2,1)S(1)}, bf16[1024,128]{1,0:T(8,128)(2,1)S(1)}, u32[]{:S(2)}, u32[]{:S(2)}) %collective-permute-start.28) | collective-permute-done | bytes 262176 | tf_op jit(solution)/shard_map/ppermute | solution.py:14
  244.2 42.8 %collective-permute-start.29 = (bf16[1024,128]{1,0:T(8,128)(2,1)S(1)}, bf16[1024,128]{1,0:T(8,128)(2,1)S(1)}, u32[]{:S(2)}, u32[]{:S(2)}) collective-permute-start(bf16[1024,128]{1,0:T(8,128)(2,1)S(1)} %get-tuple-element.231), channel_id=1, source_target_pairs={{0,128},{2,130},{4,132},{6,134},{8,136},{10,138},{12,140},{14,142}... | collective-permute-start | bytes 786440 | tf_op jit(solution)/shard_map/ppermute | solution.py:14
  287.2 5.5 %collective-permute-start.20 = (bf16[1024,128]{1,0:T(8,128)(2,1)S(1)}, bf16[1024,128]{1,0:T(8,128)(2,1)S(1)}, u32[]{:S(2)}, u32[]{:S(2)}) collective-permute-start(bf16[1024,128]{1,0:T(8,128)(2,1)S(1)} %get-tuple-element.233), channel_id=1, source_target_pairs={{0,128},{2,130},{4,132},{6,134},{8,136},{10,138},{12,140},{14,142}... | collective-permute-start | bytes 786440 | tf_op jit(solution)/shard_map/ppermute | solution.py:14
  292.7 13.7 %collective-permute-done.29 = bf16[1024,128]{1,0:T(8,128)(2,1)S(1)} collective-permute-done((bf16[1024,128]{1,0:T(8,128)(2,1)S(1)}, bf16[1024,128]{1,0:T(8,128)(2,1)S(1)}, u32[]{:S(2)}, u32[]{:S(2)}) %collective-permute-start.29) | collective-permute-done | bytes 262176 | tf_op jit(solution)/shard_map/ppermute | solution.py:14
  306.4 1.9 collective-permute-start.30
  308.3 3.7 collective-permute-done.20
  312.1 1.9 collective-permute-start.21
  314.0 14.8 %collective-permute-done.30 = bf16[1024,128]{1,0:T(8,128)(2,1)S(1)} collective-permute-done((bf16[1024,128]{1,0:T(8,128)(2,1)S(1)}, bf16[1024,128]{1,0:T(8,128)(2,1)S(1)}, u32[]{:S(2)}, u32[]{:S(2)}) %collective-permute-start.30) | collective-permute-done | bytes 262176 | tf_op jit(solution)/shard_map/ppermute | solution.py:14
  328.9 1.9 collective-permute-start.31
  330.8 3.7 collective-permute-done.21
  336.4 3.7 collective-permute-done.31
  342.0 3.7 collective-permute-done.22
  345.7 1.9 collective-permute-start.23
  347.6 3.1 collective-permute-done.32
  350.8 1.9 collective-permute-start.33
  352.7 3.8 collective-permute-done.23
  359.1 2.6 collective-permute-start.34
  361.7 2.3 collective-permute-done.24
  364.0 2.3 collective-permute-start.25
  366.3 4.7 %collective-permute-start.27 = (bf16[1024,128]{1,0:T(8,128)(2,1)S(1)}, bf16[1024,128]{1,0:T(8,128)(2,1)S(1)}, u32[]{:S(2)}, u32[]{:S(2)}) collective-permute-start(bf16[1024,128]{1,0:T(8,128)(2,1)S(1)} %get-tuple-element.232), channel_id=1, source_target_pairs={{2,0},{4,2},{6,4},{8,6},{10,8},{12,10},{14,12},{16,14},{18,16},{20... | collective-permute-start | bytes 786440 | tf_op jit(solution)/shard_map/ppermute | solution.py:10
  371.1 2.8 collective-permute-start.35
  373.8 1.9 collective-permute-start.18
  375.8 3.1 collective-permute-start.26
  380.9 2.1 collective-permute-done.18
  (118 shorter events, 28.0 us)
Async XLA Ops:
  0.6 11.4 %collective-permute-start.10 = (bf16[1024,128]{1,0:T(8,128)(2,1)}, bf16[1024,128]{1,0:T(8,128)(2,1)S(1)}, u32[]{:S(2)}, u32[]{:S(2)}) collective-permute-start(bf16[1024,128]{1,0:T(8,128)(2,1)} %bitcast.94), channel_id=1, source_target_pairs={{0,2},{2,0},{4,6},{6,4},{8,10},{10,8},{12,14},{14,12},{16,18},{18,... | collective-permute-start | bytes 786440 | tf_op jit(solution)/shard_map/ppermute | solution.py:14
  9.4 5.6 %collective-permute-start.1 = (bf16[1024,128]{1,0:T(8,128)(2,1)}, bf16[1024,128]{1,0:T(8,128)(2,1)S(1)}, u32[]{:S(2)}, u32[]{:S(2)}) collective-permute-start(bf16[1024,128]{1,0:T(8,128)(2,1)} %bitcast.97), channel_id=1, source_target_pairs={{0,2},{2,0},{4,6},{6,4},{8,10},{10,8},{12,14},{14,12},{16,18},{18,... | collective-permute-start | bytes 786440 | tf_op jit(solution)/shard_map/ppermute | solution.py:14
  13.0 10.8 %collective-permute-start.11 = (bf16[1024,128]{1,0:T(8,128)(2,1)S(1)}, bf16[1024,128]{1,0:T(8,128)(2,1)S(1)}, u32[]{:S(2)}, u32[]{:S(2)}) collective-permute-start(bf16[1024,128]{1,0:T(8,128)(2,1)S(1)} %broadcast_select_fusion), channel_id=1, source_target_pairs={{0,4},{2,6},{4,0},{6,2},{8,12},{10,14},{12,8},{14,10},{16,20},{18,... | collective-permute-start | bytes 786440 | tf_op jit(solution)/shard_map/ppermute | solution.py:14
  16.0 13.4 %collective-permute-start.2 = (bf16[1024,128]{1,0:T(8,128)(2,1)S(1)}, bf16[1024,128]{1,0:T(8,128)(2,1)S(1)}, u32[]{:S(2)}, u32[]{:S(2)}) collective-permute-start(bf16[1024,128]{1,0:T(8,128)(2,1)S(1)} %broadcast_select_fusion.1), channel_id=1, source_target_pairs={{0,4},{2,6},{4,0},{6,2},{8,12},{10,14},{12,8},{14,10},{16,20},{18,... | collective-permute-start | bytes 786440 | tf_op jit(solution)/shard_map/ppermute | solution.py:14
  23.8 7.5 %collective-permute-start.12 = (bf16[1024,128]{1,0:T(8,128)(2,1)S(1)}, bf16[1024,128]{1,0:T(8,128)(2,1)S(1)}, u32[]{:S(2)}, u32[]{:S(2)}) collective-permute-start(bf16[1024,128]{1,0:T(8,128)(2,1)S(1)} %broadcast_select_fusion.4), channel_id=1, source_target_pairs={{0,8},{2,10},{4,12},{6,14},{8,0},{10,2},{12,4},{14,6},{16,24},{18,... | collective-permute-start | bytes 786440 | tf_op jit(solution)/shard_map/ppermute | solution.py:14
  25.8 46.5 %copy-start.5 = (bf16[1,1024,128]{2,1,0:T(8,128)(2,1)S(1)}, bf16[1,1024,128]{2,1,0:T(8,128)(2,1)}, u32[]{:S(2)}) copy-start(bf16[1,1024,128]{2,1,0:T(8,128)(2,1)} %param.11) | copy-start | bytes 786436
  25.8 67.5 %copy-start.6 = (bf16[1,1024,128]{2,1,0:T(8,128)(2,1)S(1)}, bf16[1,1024,128]{2,1,0:T(8,128)(2,1)}, u32[]{:S(2)}) copy-start(bf16[1,1024,128]{2,1,0:T(8,128)(2,1)} %param.10) | copy-start | bytes 786436
  29.4 8.3 %collective-permute-start.3 = (bf16[1024,128]{1,0:T(8,128)(2,1)S(1)}, bf16[1024,128]{1,0:T(8,128)(2,1)S(1)}, u32[]{:S(2)}, u32[]{:S(2)}) collective-permute-start(bf16[1024,128]{1,0:T(8,128)(2,1)S(1)} %broadcast_select_fusion.5), channel_id=1, source_target_pairs={{0,8},{2,10},{4,12},{6,14},{8,0},{10,2},{12,4},{14,6},{16,24},{18,... | collective-permute-start | bytes 786440 | tf_op jit(solution)/shard_map/ppermute | solution.py:14
  31.4 10.1 %collective-permute-start.13 = (bf16[1024,128]{1,0:T(8,128)(2,1)S(1)}, bf16[1024,128]{1,0:T(8,128)(2,1)S(1)}, u32[]{:S(2)}, u32[]{:S(2)}) collective-permute-start(bf16[1024,128]{1,0:T(8,128)(2,1)S(1)} %broadcast_select_fusion.8), channel_id=1, source_target_pairs={{0,16},{2,18},{4,20},{6,22},{8,24},{10,26},{12,28},{14,30},{16,0},... | collective-permute-start | bytes 786440 | tf_op jit(solution)/shard_map/ppermute | solution.py:14
  37.8 9.3 %collective-permute-start.4 = (bf16[1024,128]{1,0:T(8,128)(2,1)S(1)}, bf16[1024,128]{1,0:T(8,128)(2,1)S(1)}, u32[]{:S(2)}, u32[]{:S(2)}) collective-permute-start(bf16[1024,128]{1,0:T(8,128)(2,1)S(1)} %broadcast_select_fusion.9), channel_id=1, source_target_pairs={{0,16},{2,18},{4,20},{6,22},{8,24},{10,26},{12,28},{14,30},{16,0},... | collective-permute-start | bytes 786440 | tf_op jit(solution)/shard_map/ppermute | solution.py:14
  41.5 8.1 %collective-permute-start.14 = (bf16[1024,128]{1,0:T(8,128)(2,1)S(1)}, bf16[1024,128]{1,0:T(8,128)(2,1)S(1)}, u32[]{:S(2)}, u32[]{:S(2)}) collective-permute-start(bf16[1024,128]{1,0:T(8,128)(2,1)S(1)} %broadcast_select_fusion.12), channel_id=1, source_target_pairs={{0,32},{2,34},{4,36},{6,38},{8,40},{10,42},{12,44},{14,46},{16,48}... | collective-permute-start | bytes 786440 | tf_op jit(solution)/shard_map/ppermute | solution.py:14
  47.1 8.3 %collective-permute-start.5 = (bf16[1024,128]{1,0:T(8,128)(2,1)S(1)}, bf16[1024,128]{1,0:T(8,128)(2,1)S(1)}, u32[]{:S(2)}, u32[]{:S(2)}) collective-permute-start(bf16[1024,128]{1,0:T(8,128)(2,1)S(1)} %broadcast_select_fusion.13), channel_id=1, source_target_pairs={{0,32},{2,34},{4,36},{6,38},{8,40},{10,42},{12,44},{14,46},{16,48}... | collective-permute-start | bytes 786440 | tf_op jit(solution)/shard_map/ppermute | solution.py:14
  49.6 13.8 %collective-permute-start.15 = (bf16[1024,128]{1,0:T(8,128)(2,1)S(1)}, bf16[1024,128]{1,0:T(8,128)(2,1)S(1)}, u32[]{:S(2)}, u32[]{:S(2)}) collective-permute-start(bf16[1024,128]{1,0:T(8,128)(2,1)S(1)} %broadcast_select_fusion.16), channel_id=1, source_target_pairs={{0,64},{2,66},{4,68},{6,70},{8,72},{10,74},{12,76},{14,78},{16,80}... | collective-permute-start | bytes 786440 | tf_op jit(solution)/shard_map/ppermute | solution.py:14
  55.5 39.8 %collective-permute-start.6 = (bf16[1024,128]{1,0:T(8,128)(2,1)S(1)}, bf16[1024,128]{1,0:T(8,128)(2,1)S(1)}, u32[]{:S(2)}, u32[]{:S(2)}) collective-permute-start(bf16[1024,128]{1,0:T(8,128)(2,1)S(1)} %broadcast_select_fusion.17), channel_id=1, source_target_pairs={{0,64},{2,66},{4,68},{6,70},{8,72},{10,74},{12,76},{14,78},{16,80}... | collective-permute-start | bytes 786440 | tf_op jit(solution)/shard_map/ppermute | solution.py:14
  63.5 35.2 %collective-permute-start.16 = (bf16[1024,128]{1,0:T(8,128)(2,1)S(1)}, bf16[1024,128]{1,0:T(8,128)(2,1)S(1)}, u32[]{:S(2)}, u32[]{:S(2)}) collective-permute-start(bf16[1024,128]{1,0:T(8,128)(2,1)S(1)} %broadcast_select_fusion.20), channel_id=1, source_target_pairs={{0,128},{2,130},{4,132},{6,134},{8,136},{10,138},{12,140},{14,142}... | collective-permute-start | bytes 786440 | tf_op jit(solution)/shard_map/ppermute | solution.py:14
  72.3 85.8 %collective-permute-start.9 = (bf16[1024,128]{1,0:T(8,128)(2,1)S(1)}, bf16[1024,128]{1,0:T(8,128)(2,1)S(1)}, u32[]{:S(2)}, u32[]{:S(2)}) collective-permute-start(bf16[1024,128]{1,0:T(8,128)(2,1)S(1)} %bitcast.95), channel_id=1, source_target_pairs={{0,2},{2,4},{4,6},{6,8},{8,10},{10,12},{12,14},{14,16},{16,18},{18... | collective-permute-start | bytes 786440 | tf_op jit(solution)/shard_map/ppermute | solution.py:10
  93.3 74.5 %collective-permute-start = (bf16[1024,128]{1,0:T(8,128)(2,1)S(1)}, bf16[1024,128]{1,0:T(8,128)(2,1)S(1)}, u32[]{:S(2)}, u32[]{:S(2)}) collective-permute-start(bf16[1024,128]{1,0:T(8,128)(2,1)S(1)} %bitcast.98), channel_id=1, source_target_pairs={{0,2},{2,4},{4,6},{6,8},{8,10},{10,12},{12,14},{14,16},{16,18},{18... | collective-permute-start | bytes 786440 | tf_op jit(solution)/shard_map/ppermute | solution.py:10
  95.3 52.7 %collective-permute-start.7 = (bf16[1024,128]{1,0:T(8,128)(2,1)S(1)}, bf16[1024,128]{1,0:T(8,128)(2,1)S(1)}, u32[]{:S(2)}, u32[]{:S(2)}) collective-permute-start(bf16[1024,128]{1,0:T(8,128)(2,1)S(1)} %broadcast_select_fusion.21), channel_id=1, source_target_pairs={{0,128},{2,130},{4,132},{6,134},{8,136},{10,138},{12,140},{14,142}... | collective-permute-start | bytes 786440 | tf_op jit(solution)/shard_map/ppermute | solution.py:14
  98.7 59.4 %collective-permute-start.17 = (bf16[1024,128]{1,0:T(8,128)(2,1)S(1)}, bf16[1024,128]{1,0:T(8,128)(2,1)S(1)}, u32[]{:S(2)}, u32[]{:S(2)}) collective-permute-start(bf16[1024,128]{1,0:T(8,128)(2,1)S(1)} %broadcast_select_fusion.24), channel_id=1, source_target_pairs={{0,256},{2,258},{4,260},{6,262},{8,264},{10,266},{12,268},{14,270}... | collective-permute-start | bytes 786440 | tf_op jit(solution)/shard_map/ppermute | solution.py:14
  148.0 19.7 %collective-permute-start.8 = (bf16[1024,128]{1,0:T(8,128)(2,1)S(1)}, bf16[1024,128]{1,0:T(8,128)(2,1)S(1)}, u32[]{:S(2)}, u32[]{:S(2)}) collective-permute-start(bf16[1024,128]{1,0:T(8,128)(2,1)S(1)} %broadcast_select_fusion.25), channel_id=1, source_target_pairs={{0,256},{2,258},{4,260},{6,262},{8,264},{10,266},{12,268},{14,270}... | collective-permute-start | bytes 786440 | tf_op jit(solution)/shard_map/ppermute | solution.py:14
  167.9 19.2 %copy-start.3 = (bf16[1,1024,128]{2,1,0:T(8,128)(2,1)S(1)}, bf16[1,1024,128]{2,1,0:T(8,128)(2,1)}, u32[]{:S(2)}) copy-start(bf16[1,1024,128]{2,1,0:T(8,128)(2,1)} %param.12) | copy-start | bytes 786436
  187.0 1.0 copy-start.4
  188.0 0.9 copy-start.1
  188.0 1.1 copy-start.7
  192.3 3.2 copy-start.9
  197.6 0.7 copy-start.10
  198.3 4.2 %copy-start.2 = (bf16[3072,128]{1,0:T(8,128)(2,1)S(1)}, bf16[3072,128]{1,0:T(8,128)(2,1)}, u32[]{:S(2)}) copy-start(bf16[3072,128]{1,0:T(8,128)(2,1)} %copy-done.1) | copy-start | bytes 2359300 | tf_op jit(solution)/shard_map/while
  198.3 4.2 %copy-start.8 = (bf16[3072,128]{1,0:T(8,128)(2,1)S(1)}, bf16[3072,128]{1,0:T(8,128)(2,1)}, u32[]{:S(2)}) copy-start(bf16[3072,128]{1,0:T(8,128)(2,1)} %copy-done.7) | copy-start | bytes 2359300 | tf_op jit(solution)/shard_map/while
  202.6 0.9 copy-start.1
  202.6 1.1 copy-start.7
  206.8 3.7 copy-start.9
  212.7 0.7 copy-start.10
  213.5 4.7 %copy-start.2 = (bf16[3072,128]{1,0:T(8,128)(2,1)S(1)}, bf16[3072,128]{1,0:T(8,128)(2,1)}, u32[]{:S(2)}) copy-start(bf16[3072,128]{1,0:T(8,128)(2,1)} %copy-done.1) | copy-start | bytes 2359300 | tf_op jit(solution)/shard_map/while
  213.5 4.7 %copy-start.8 = (bf16[3072,128]{1,0:T(8,128)(2,1)S(1)}, bf16[3072,128]{1,0:T(8,128)(2,1)}, u32[]{:S(2)}) copy-start(bf16[3072,128]{1,0:T(8,128)(2,1)} %copy-done.7) | copy-start | bytes 2359300 | tf_op jit(solution)/shard_map/while
  218.1 13.8 %copy-start = (f32[3072,128]{1,0:T(8,128)S(1)}, f32[3072,128]{1,0:T(8,128)}, u32[]{:S(2)}) copy-start(f32[3072,128]{1,0:T(8,128)} %get-tuple-element.156) | copy-start | bytes 4718596
  219.8 24.4 %collective-permute-start.28 = (bf16[1024,128]{1,0:T(8,128)(2,1)S(1)}, bf16[1024,128]{1,0:T(8,128)(2,1)S(1)}, u32[]{:S(2)}, u32[]{:S(2)}) collective-permute-start(bf16[1024,128]{1,0:T(8,128)(2,1)S(1)} %slice.31), channel_id=1, source_target_pairs={{0,256},{2,258},{4,260},{6,262},{8,264},{10,266},{12,268},{14,270}... | collective-permute-start | bytes 786440 | tf_op jit(solution)/shard_map/ppermute | solution.py:14
  232.1 55.0 %collective-permute-start.19 = (bf16[1024,128]{1,0:T(8,128)(2,1)S(1)}, bf16[1024,128]{1,0:T(8,128)(2,1)S(1)}, u32[]{:S(2)}, u32[]{:S(2)}) collective-permute-start(bf16[1024,128]{1,0:T(8,128)(2,1)S(1)} %slice.29), channel_id=1, source_target_pairs={{0,256},{2,258},{4,260},{6,262},{8,264},{10,266},{12,268},{14,270}... | collective-permute-start | bytes 786440 | tf_op jit(solution)/shard_map/ppermute | solution.py:14
  244.2 62.1 %collective-permute-start.29 = (bf16[1024,128]{1,0:T(8,128)(2,1)S(1)}, bf16[1024,128]{1,0:T(8,128)(2,1)S(1)}, u32[]{:S(2)}, u32[]{:S(2)}) collective-permute-start(bf16[1024,128]{1,0:T(8,128)(2,1)S(1)} %get-tuple-element.231), channel_id=1, source_target_pairs={{0,128},{2,130},{4,132},{6,134},{8,136},{10,138},{12,140},{14,142}... | collective-permute-start | bytes 786440 | tf_op jit(solution)/shard_map/ppermute | solution.py:14
  287.2 24.9 %collective-permute-start.20 = (bf16[1024,128]{1,0:T(8,128)(2,1)S(1)}, bf16[1024,128]{1,0:T(8,128)(2,1)S(1)}, u32[]{:S(2)}, u32[]{:S(2)}) collective-permute-start(bf16[1024,128]{1,0:T(8,128)(2,1)S(1)} %get-tuple-element.233), channel_id=1, source_target_pairs={{0,128},{2,130},{4,132},{6,134},{8,136},{10,138},{12,140},{14,142}... | collective-permute-start | bytes 786440 | tf_op jit(solution)/shard_map/ppermute | solution.py:14
  306.4 22.4 %collective-permute-start.30 = (bf16[1024,128]{1,0:T(8,128)(2,1)S(1)}, bf16[1024,128]{1,0:T(8,128)(2,1)S(1)}, u32[]{:S(2)}, u32[]{:S(2)}) collective-permute-start(bf16[1024,128]{1,0:T(8,128)(2,1)S(1)} %broadcast_select_fusion.22), channel_id=1, source_target_pairs={{0,64},{2,66},{4,68},{6,70},{8,72},{10,74},{12,76},{14,78},{16,80}... | collective-permute-start | bytes 786440 | tf_op jit(solution)/shard_map/ppermute | solution.py:14
  312.1 22.4 %collective-permute-start.21 = (bf16[1024,128]{1,0:T(8,128)(2,1)S(1)}, bf16[1024,128]{1,0:T(8,128)(2,1)S(1)}, u32[]{:S(2)}, u32[]{:S(2)}) collective-permute-start(bf16[1024,128]{1,0:T(8,128)(2,1)S(1)} %broadcast_select_fusion.23), channel_id=1, source_target_pairs={{0,64},{2,66},{4,68},{6,70},{8,72},{10,74},{12,76},{14,78},{16,80}... | collective-permute-start | bytes 786440 | tf_op jit(solution)/shard_map/ppermute | solution.py:14
  328.9 11.2 %collective-permute-start.31 = (bf16[1024,128]{1,0:T(8,128)(2,1)S(1)}, bf16[1024,128]{1,0:T(8,128)(2,1)S(1)}, u32[]{:S(2)}, u32[]{:S(2)}) collective-permute-start(bf16[1024,128]{1,0:T(8,128)(2,1)S(1)} %broadcast_select_fusion.18), channel_id=1, source_target_pairs={{0,32},{2,34},{4,36},{6,38},{8,40},{10,42},{12,44},{14,46},{16,48}... | collective-permute-start | bytes 786440 | tf_op jit(solution)/shard_map/ppermute | solution.py:14
  334.5 11.2 %collective-permute-start.22 = (bf16[1024,128]{1,0:T(8,128)(2,1)S(1)}, bf16[1024,128]{1,0:T(8,128)(2,1)S(1)}, u32[]{:S(2)}, u32[]{:S(2)}) collective-permute-start(bf16[1024,128]{1,0:T(8,128)(2,1)S(1)} %broadcast_select_fusion.19), channel_id=1, source_target_pairs={{0,32},{2,34},{4,36},{6,38},{8,40},{10,42},{12,44},{14,46},{16,48}... | collective-permute-start | bytes 786440 | tf_op jit(solution)/shard_map/ppermute | solution.py:14
  340.1 10.7 %collective-permute-start.32 = (bf16[1024,128]{1,0:T(8,128)(2,1)S(1)}, bf16[1024,128]{1,0:T(8,128)(2,1)S(1)}, u32[]{:S(2)}, u32[]{:S(2)}) collective-permute-start(bf16[1024,128]{1,0:T(8,128)(2,1)S(1)} %broadcast_select_fusion.14), channel_id=1, source_target_pairs={{0,16},{2,18},{4,20},{6,22},{8,24},{10,26},{12,28},{14,30},{16,0},... | collective-permute-start | bytes 786440 | tf_op jit(solution)/shard_map/ppermute | solution.py:14
  345.7 10.8 %collective-permute-start.23 = (bf16[1024,128]{1,0:T(8,128)(2,1)S(1)}, bf16[1024,128]{1,0:T(8,128)(2,1)S(1)}, u32[]{:S(2)}, u32[]{:S(2)}) collective-permute-start(bf16[1024,128]{1,0:T(8,128)(2,1)S(1)} %broadcast_select_fusion.15), channel_id=1, source_target_pairs={{0,16},{2,18},{4,20},{6,22},{8,24},{10,26},{12,28},{14,30},{16,0},... | collective-permute-start | bytes 786440 | tf_op jit(solution)/shard_map/ppermute | solution.py:14
  350.8 8.2 %collective-permute-start.33 = (bf16[1024,128]{1,0:T(8,128)(2,1)S(1)}, bf16[1024,128]{1,0:T(8,128)(2,1)S(1)}, u32[]{:S(2)}, u32[]{:S(2)}) collective-permute-start(bf16[1024,128]{1,0:T(8,128)(2,1)S(1)} %broadcast_select_fusion.10), channel_id=1, source_target_pairs={{0,8},{2,10},{4,12},{6,14},{8,0},{10,2},{12,4},{14,6},{16,24},{18,... | collective-permute-start | bytes 786440 | tf_op jit(solution)/shard_map/ppermute | solution.py:14
  356.5 7.4 %collective-permute-start.24 = (bf16[1024,128]{1,0:T(8,128)(2,1)S(1)}, bf16[1024,128]{1,0:T(8,128)(2,1)S(1)}, u32[]{:S(2)}, u32[]{:S(2)}) collective-permute-start(bf16[1024,128]{1,0:T(8,128)(2,1)S(1)} %broadcast_select_fusion.11), channel_id=1, source_target_pairs={{0,8},{2,10},{4,12},{6,14},{8,0},{10,2},{12,4},{14,6},{16,24},{18,... | collective-permute-start | bytes 786440 | tf_op jit(solution)/shard_map/ppermute | solution.py:14
  359.1 11.9 %collective-permute-start.34 = (bf16[1024,128]{1,0:T(8,128)(2,1)S(1)}, bf16[1024,128]{1,0:T(8,128)(2,1)S(1)}, u32[]{:S(2)}, u32[]{:S(2)}) collective-permute-start(bf16[1024,128]{1,0:T(8,128)(2,1)S(1)} %broadcast_select_fusion.6), channel_id=1, source_target_pairs={{0,4},{2,6},{4,0},{6,2},{8,12},{10,14},{12,8},{14,10},{16,20},{18,... | collective-permute-start | bytes 786440 | tf_op jit(solution)/shard_map/ppermute | solution.py:14
  364.0 11.8 %collective-permute-start.25 = (bf16[1024,128]{1,0:T(8,128)(2,1)S(1)}, bf16[1024,128]{1,0:T(8,128)(2,1)S(1)}, u32[]{:S(2)}, u32[]{:S(2)}) collective-permute-start(bf16[1024,128]{1,0:T(8,128)(2,1)S(1)} %broadcast_select_fusion.7), channel_id=1, source_target_pairs={{0,4},{2,6},{4,0},{6,2},{8,12},{10,14},{12,8},{14,10},{16,20},{18,... | collective-permute-start | bytes 786440 | tf_op jit(solution)/shard_map/ppermute | solution.py:14
  366.3 12.7 %collective-permute-start.27 = (bf16[1024,128]{1,0:T(8,128)(2,1)S(1)}, bf16[1024,128]{1,0:T(8,128)(2,1)S(1)}, u32[]{:S(2)}, u32[]{:S(2)}) collective-permute-start(bf16[1024,128]{1,0:T(8,128)(2,1)S(1)} %get-tuple-element.232), channel_id=1, source_target_pairs={{2,0},{4,2},{6,4},{8,6},{10,8},{12,10},{14,12},{16,14},{18,16},{20... | collective-permute-start | bytes 786440 | tf_op jit(solution)/shard_map/ppermute | solution.py:10
  371.1 8.0 %collective-permute-start.35 = (bf16[1024,128]{1,0:T(8,128)(2,1)S(1)}, bf16[1024,128]{1,0:T(8,128)(2,1)S(1)}, u32[]{:S(2)}, u32[]{:S(2)}) collective-permute-start(bf16[1024,128]{1,0:T(8,128)(2,1)S(1)} %broadcast_select_fusion.2), channel_id=1, source_target_pairs={{0,2},{2,0},{4,6},{6,4},{8,10},{10,8},{12,14},{14,12},{16,18},{18,... | collective-permute-start | bytes 786440 | tf_op jit(solution)/shard_map/ppermute | solution.py:14
  373.8 9.2 %collective-permute-start.18 = (bf16[1024,128]{1,0:T(8,128)(2,1)S(1)}, bf16[1024,128]{1,0:T(8,128)(2,1)S(1)}, u32[]{:S(2)}, u32[]{:S(2)}) collective-permute-start(bf16[1024,128]{1,0:T(8,128)(2,1)S(1)} %get-tuple-element.234), channel_id=1, source_target_pairs={{2,0},{4,2},{6,4},{8,6},{10,8},{12,10},{14,12},{16,14},{18,16},{20... | collective-permute-start | bytes 786440 | tf_op jit(solution)/shard_map/ppermute | solution.py:10
  375.8 7.2 %collective-permute-start.26 = (bf16[1024,128]{1,0:T(8,128)(2,1)S(1)}, bf16[1024,128]{1,0:T(8,128)(2,1)S(1)}, u32[]{:S(2)}, u32[]{:S(2)}) collective-permute-start(bf16[1024,128]{1,0:T(8,128)(2,1)S(1)} %broadcast_select_fusion.3), channel_id=1, source_target_pairs={{0,2},{2,0},{4,6},{6,4},{8,10},{10,8},{12,14},{14,12},{16,18},{18,... | collective-permute-start | bytes 786440 | tf_op jit(solution)/shard_map/ppermute | solution.py:14
where the time goes:
time: 388 us; the launch traced here: 384 us
  starting transfers between devices  196 us (51%)
  waiting for transfers between devices  128 us (33%)
  matrix products  35.2 us (9%)
  other arithmetic  16.6 us (4%)
  local copies, waits for them, and re-layouts  5.73 us (1%)
    ppermute x32, starting transfers between devices, from_partner(): lax.ppermute(x, axis, [(i, i ^ 1 << stride) for i in range(lax.axis_size(...  166 us
    ppermute x32, waiting for transfers between devices, from_partner(): lax.ppermute(x, axis, [(i, i ^ 1 << stride) for i in range(lax.axis_size(...  126 us
    ppermute x4, starting transfers between devices, from_behind(): return lax.ppermute(block, axis, route)  29.5 us
    dot_general x2, matrix products, backward_rows(): jnp.einsum('qk,qd->kd', weights_bf, grad_block, preferred_element_type=jn...  8.88 us
  transfers between devices with their start and end apart: 36, of which 21 were waited for; matrix products, arithmetic and copies ran while one was open for 1% of the time, Pallas kernels for 0%

commit v1 on v0

v1 whole, which is shorter than its diff:
```python
import functools
import math

import jax
import jax.numpy as jnp
from jax import lax
from jax.experimental import pallas as pl
from jax.experimental.pallas import tpu as pltpu
from jax.sharding import PartitionSpec as P

F32 = jnp.float32
BF16 = jnp.bfloat16
NT = (((1,), (1,)), ((), ()))
NN = (((1,), (0,)), ((), ()))
CHUNK = 256
INF = float("inf")
VMEM_LIMIT = 48 * 1024 * 1024


def dot(a, b, dims=NN):
    return lax.dot_general(a, b, dims, preferred_element_type=F32)


def chunks(rows):
    return [slice(at, at + CHUNK) for at in range(0, rows, CHUNK)]


def causal(scores, first):
    kpos = lax.broadcasted_iota(jnp.int32, scores.shape, 0)
    qpos = lax.broadcasted_iota(jnp.int32, scores.shape, 1) + first
    return jnp.where(kpos <= qpos, scores, -INF)


def call(kernel, out_shape, n_in, scalars=0):
    vmem = pl.BlockSpec(memory_space=pltpu.VMEM)
    smem = pl.BlockSpec(memory_space=pltpu.SMEM)
    return pl.pallas_call(
        kernel,
        out_shape=out_shape,
        in_specs=[smem] * scalars + [vmem] * n_in,
        out_specs=jax.tree.map(lambda _: vmem, out_shape),
        compiler_params=pltpu.CompilerParams(vmem_limit_bytes=VMEM_LIMIT),
    )


def thirds(x):
    high = x.astype(BF16).astype(F32)
    middle = (x - high).astype(BF16).astype(F32)
    return high, middle, x - high - middle


def stats_kernel(scale, at, route, q_ref, g_ref, k_ref, v_ref, kb_ref, vb_ref, out_ref, notes_ref, rows_ref):
    leading = at[0] == 0
    parts = q_ref.shape[0] // CHUNK
    rows_ref[...] = jnp.full(rows_ref.shape, route[0].astype(F32))
    for t, cols in enumerate(chunks(q_ref.shape[0])):
        q, g = q_ref[cols], g_ref[cols]
        own = causal(dot(k_ref[: cols.stop], q, NT) * scale, cols.start)
        before = dot(kb_ref[...], q, NT) * scale
        peak_before = jnp.where(leading, -INF, jnp.max(before, 0, keepdims=True))
        peak = jnp.maximum(jnp.max(own, 0, keepdims=True), peak_before)
        own = jnp.exp2(own - peak)
        before = jnp.exp2(before - jnp.where(leading, INF, peak))
        total = jnp.sum(own, 0, keepdims=True) + jnp.sum(before, 0, keepdims=True)
        pushed = jnp.sum(own * dot(v_ref[: cols.stop], g, NT), 0, keepdims=True)
        pushed += jnp.sum(before * dot(vb_ref[...], g, NT), 0, keepdims=True)
        for kind, row in enumerate((peak + jnp.log2(total), pushed / total)):
            out_ref[kind : kind + 1, cols] = row
            for i, third in enumerate(thirds(row)):
                to = (3 * kind + i) * parts + t
                rows_ref[to : to + 1] = third
    notes_ref[...] = rows_ref[...].T.astype(BF16)


def read_notes(notes_ref, parts):
    rows = notes_ref[...].astype(F32).T
    sums = [sum(rows[(3 * kind + i) * parts : (3 * kind + i + 1) * parts] for i in range(3)) for kind in range(2)]
    return [[total[t : t + 1] for t in range(parts)] for total in sums]


def joined(elsewhere, scores):
    peak = jnp.max(scores, 0, keepdims=True)
    raw = jnp.exp2(scores - peak)
    here = peak + jnp.log2(jnp.sum(raw, 0, keepdims=True))
    top = jnp.maximum(elsewhere, here)
    log_total = top + jnp.log2(jnp.exp2(elsewhere - top) + jnp.exp2(here - top))
    return raw * jnp.exp2(peak - log_total), log_total, jnp.exp2(elsewhere - log_total)


def query_kernel(
    scale, factor, at, q_ref, g_ref, k_ref, v_ref, kb_ref, vb_ref, kp_ref, vp_ref, stats_ref,
    att_ref, dq_ref, dk_ref, dv_ref, dkb_ref, dvb_ref, dkb_acc, dvb_acc,
):
    leading = at[0] == 0
    k_t, kb_t, kp_t = k_ref[...].T, kb_ref[...].T, kp_ref[...].T
    v_t, vb_t, vp_t = v_ref[...].T, vb_ref[...].T, vp_ref[...].T
    dk_ref[...] = jnp.zeros_like(dk_ref)
    dv_ref[...] = jnp.zeros_like(dv_ref)
    dkb_acc[...] = jnp.zeros_like(dkb_acc)
    dvb_acc[...] = jnp.zeros_like(dvb_acc)
    for cols in chunks(q_ref.shape[0]):
        q, g = q_ref[cols], g_ref[cols]
        keys = slice(0, cols.stop)
        w_partner, log_total, _ = joined(stats_ref[0:1, cols], dot(kp_ref[...], q, NT) * scale)
        w_partner = w_partner.astype(BF16)
        w_own = jnp.exp2(causal(dot(k_ref[keys], q, NT) * scale, cols.start) - log_total).astype(BF16)
        log_before = jnp.where(leading, INF, log_total)
        w_before = jnp.exp2(dot(kb_ref[...], q, NT) * scale - log_before).astype(BF16)
        attended = dot(vp_t, w_partner) + dot(v_t[:, keys], w_own) + dot(vb_t, w_before)
        attended = attended.astype(BF16).astype(F32)
        att_ref[cols] = attended.T.astype(BF16)
        drift = jnp.sum(attended * g.astype(F32).T, 0, keepdims=True)

        def shape(weights, v):
            return (weights.astype(F32) * (dot(v, g, NT) - drift)).astype(BF16)

        s_before = shape(w_before, vb_ref[...])
        dkb_acc[...] += dot(s_before, q)
        dvb_acc[...] += dot(w_before, g)
        s_own = shape(w_own, v_ref[keys])
        dk_ref[keys] += dot(s_own, q)
        dv_ref[keys] += dot(w_own, g)
        s_partner = shape(w_partner, vp_ref[...])
        dq = dot(kp_t, s_partner) + dot(k_t[:, keys], s_own) + dot(kb_t, s_before)
        dq_ref[cols] = (dq * factor).T.astype(BF16)
    dk_ref[...] *= factor
    dkb_ref[...] = (dkb_acc[...] * factor).astype(BF16)
    dvb_ref[...] = dvb_acc[...].astype(BF16)


def key_kernel(scale, factor, q_ref, g_ref, k_ref, v_ref, notes_ref, dk_own, dv_own, dk_ref, dv_ref, dk_acc, dv_acc):
    dk_acc[...] = jnp.zeros_like(dk_acc)
    dv_acc[...] = jnp.zeros_like(dv_acc)
    elsewhere, pushed_there = read_notes(notes_ref, q_ref.shape[0] // CHUNK)
    for t, cols in enumerate(chunks(q_ref.shape[0])):
        q, g = q_ref[cols], g_ref[cols]
        weights, _, share = joined(elsewhere[t], dot(k_ref[...], q, NT) * scale)
        pushed = dot(v_ref[...], g, NT)
        drift = share * pushed_there[t] + jnp.sum(weights * pushed, 0, keepdims=True)
        weights = weights.astype(BF16)
        shaped = (weights.astype(F32) * (pushed - drift)).astype(BF16)
        dk_acc[...] += dot(shaped, q)
        dv_acc[...] += dot(weights, g)
    dk_ref[...] = dk_own[...] + (dk_acc[...] * factor).astype(BF16).astype(F32)
    dv_ref[...] = dv_own[...] + dv_acc[...].astype(BF16).astype(F32)


def partner_kernel(route_ref, partner_ref, inverse_ref):
    route = route_ref[...]
    n = route.shape[1]
    lane = lax.broadcasted_iota(jnp.int32, route.shape, 1)

    def section(holder, s):
        far = 1 << s
        across = jnp.where((lane >> s) & 1 == 1, pltpu.roll(holder, far, 1), pltpu.roll(holder, n - far, 1))
        return jnp.where((route >> s) & 1 == 1, across, holder)

    sections = range(n.bit_length() - 1)
    partner_ref[...] = functools.reduce(section, sections, lane)
    inverse_ref[...] = functools.reduce(section, reversed(sections), lane)


def reorder_kernel(partner_ref, inverse_ref, x_ref, out_ref):
    keep = x_ref.shape[1] // 2

    def body(d, carry):
        out_ref[d, :keep] = x_ref[partner_ref[0, d], :keep]
        out_ref[d, keep:] = x_ref[inverse_ref[0, d], keep:]
        return carry

    lax.fori_loop(0, x_ref.shape[0], body, 0, unroll=8)


def shifted(x, distance):
    n = lax.axis_size("seq")
    return lax.ppermute(x, "seq", [(i, i + distance) for i in range(n) if 0 <= i + distance < n])


def local(queries, keys, values, out_grad, route):
    q, k, v, g = queries[0], keys[0], values[0], out_grad[0]
    rows, width = q.shape
    n = lax.axis_size("seq")
    me = lax.axis_index("seq")
    factor = width**-0.5
    scale = factor * math.log2(math.e)
    at = me.reshape(1)
    part = 2 * rows // n
    block = jax.ShapeDtypeStruct((rows, width), BF16)
    block32 = jax.ShapeDtypeStruct((rows, width), F32)

    vmem = pl.BlockSpec(memory_space=pltpu.VMEM)
    smem = pl.BlockSpec(memory_space=pltpu.SMEM)
    params = pltpu.CompilerParams(vmem_limit_bytes=VMEM_LIMIT)

    k_before, v_before = shifted((k, v), 1)
    stats, notes = pl.pallas_call(
        functools.partial(stats_kernel, scale),
        out_shape=(jax.ShapeDtypeStruct((2, rows), F32), jax.ShapeDtypeStruct((n, width), BF16)),
        in_specs=[smem] * 2 + [vmem] * 6,
        out_specs=(vmem, vmem),
        scratch_shapes=[pltpu.VMEM((width, n), F32)],
        compiler_params=params,
    )(at, route.reshape(1), q, g, k, v, k_before, v_before)

    def pairs(x):
        return x.reshape(n, -1, 2, width)

    spread = jnp.concatenate(
        [
            pairs(jnp.concatenate([k, v])),
            pairs(jnp.concatenate([q, g])),
            pairs(jnp.stack([notes, notes], 1)),
        ],
        1,
    )
    spread = lax.all_to_all(spread, "seq", 0, 0, tiled=True)
    routes = spread[:, -1, 0, -1].astype(jnp.int32).reshape(1, n)
    index = jax.ShapeDtypeStruct((1, n), jnp.int32)
    partner, inverse = call(partner_kernel, (index, index), 1)(routes)
    moved = call(reorder_kernel, jax.ShapeDtypeStruct(spread.shape, BF16), 1, 2)(partner, inverse, spread)
    moved = lax.all_to_all(moved, "seq", 0, 0, tiled=True)
    kv = moved[:, : part // 2].reshape(2 * rows, width)
    qg = moved[:, part // 2 : part].reshape(2 * rows, width)
    notes = moved[:, -1, 0]

    acc = [pltpu.VMEM((rows, width), F32)] * 2
    attended, query_grad, dk, dv, dk_before, dv_before = pl.pallas_call(
        functools.partial(query_kernel, scale, factor),
        out_shape=(block, block, block32, block32, block, block),
        in_specs=[smem] + [vmem] * 9,
        out_specs=(vmem,) * 6,
        scratch_shapes=acc,
        compiler_params=params,
    )(at, q, g, k, v, k_before, v_before, kv[:rows], kv[rows:], stats)
    dk_back, dv_back = shifted((dk_before, dv_before), -1)
    dk, dv = pl.pallas_call(
        functools.partial(key_kernel, scale, factor),
        out_shape=(block32, block32),
        in_specs=[vmem] * 7,
        out_specs=(vmem,) * 2,
        scratch_shapes=acc,
        compiler_params=params,
    )(qg[:rows], qg[rows:], k, v, notes, dk, dv)
    key_grad = (dk + dk_back.astype(F32)).astype(BF16)
    value_grad = (dv + dv_back.astype(F32)).astype(BF16)
    return attended[None], query_grad[None], key_grad[None], value_grad[None]


def solution(mesh):
    whole = P("head", "seq", None)
    return jax.shard_map(
        local,
        mesh=mesh,
        in_specs=(whole,) * 4 + (P("head", "seq"),),
        out_specs=(whole,) * 4,
        check_vma=False,
    )
```

time: 388 us -> 208 us (0.54); the launches traced: 384 us -> 208 us
  starting transfers between devices: 196 us -> 12.2 us
  blocking collectives: 0 us -> 159 us
  waiting for transfers between devices: 128 us -> 4.62 us
  matrix products: 35.2 us -> 0 us
  Pallas kernels: 0 us -> 20.3 us
  other arithmetic: 16.6 us -> 9.55 us
  local copies, waits for them, and re-layouts: 5.73 us -> 0.94 us
    ppermute x36 -> x4, starting transfers between devices: 196 us -> 12.2 us  [shifted(): lax.ppermute(x, 'seq', [(i, i + distance) for i in range(n) if 0 <= i + d...]
    all_to_all x0 -> x2, blocking collectives: none -> 159 us  [the longest x1 87.5 us: local(): spread = lax.all_to_all(spread, 'seq', 0, 0, tiled=True)]
    ppermute x36 -> x4, waiting for transfers between devices: 128 us -> 4.62 us  [shifted(): lax.ppermute(x, 'seq', [(i, i + distance) for i in range(n) if 0 <= i + d...]
    dot_general x12 -> x0, matrix products: 35.2 us -> none  [the longest x2 8.88 us: backward_rows(): jnp.einsum('qk,qd->kd', weights_bf, grad_block, preferred_element_type=jn...]
    pallas_call x0 -> x5, Pallas kernels: none -> 20.3 us  [the longest x1 10.3 us: local(): pl.pallas_call(functools.partial(query_kernel, scale, factor), out_shape=...]
    dynamic_update_slice x2 -> x0, other arithmetic: 5.69 us -> none  [local(): lax.map(forward_rows, (query_blocks, offsets))]
    convert_element_type x0 -> x1, other arithmetic: none -> 4.83 us  [local(): routes = spread[:, -1, 0, -1].astype(jnp.int32).reshape(1, n)]
  transfers between devices with their start and end apart: 36 -> 4, of which waited for: 21 -> 2; matrix products, arithmetic and copies ran while one was open for 1% -> 1% of each run, Pallas kernels for 0% -> 2%
where the time goes in v1:
time: 208 us
  blocking collectives  159 us (76%)
  Pallas kernels  20.3 us (10%)
  starting transfers between devices  12.2 us (6%)
  other arithmetic  9.55 us (5%)
  waiting for transfers between devices  4.62 us (2%)
    all_to_all x1, blocking collectives, local(): spread = lax.all_to_all(spread, 'seq', 0, 0, tiled=True)  87.5 us
    all_to_all x1, blocking collectives, local(): moved = lax.all_to_all(moved, 'seq', 0, 0, tiled=True)  71.5 us
    ppermute x4, starting transfers between devices, shifted(): lax.ppermute(x, 'seq', [(i, i + distance) for i in range(n) if 0 <= i + d...  12.2 us
    pallas_call x1, Pallas kernels, local(): pl.pallas_call(functools.partial(query_kernel, scale, factor), out_shape=...  10.3 us
    pallas_call x1, Pallas kernels, local(): pl.pallas_call(functools.partial(key_kernel, scale, factor), out_shape=(b...  5.06 us
    convert_element_type x1, other arithmetic, local(): routes = spread[:, -1, 0, -1].astype(jnp.int32).reshape(1, n)  4.83 us
    ppermute x4, waiting for transfers between devices, shifted(): lax.ppermute(x, 'seq', [(i, i + distance) for i in range(n) if 0 <= i + d...  4.62 us
  transfers between devices with their start and end apart: 4, of which 2 were waited for; matrix products, arithmetic and copies ran while one was open for 1% of the time, Pallas kernels for 2%

profile of v1, /device:TPU:1, one launch (start us, length us, event | category | flops | bytes accessed | tf_op | source)
XLA Modules:
  0.0 208.1 jit_solution(11340040737797412895)
XLA Ops:
  0.6 0.0 copy-start
  0.6 0.0 copy-start.1
  0.7 0.0 copy-start.3
  0.7 0.0 copy-start.2
  0.7 6.2 %collective-permute-start = (bf16[1024,128]{1,0:T(8,128)(2,1)}, bf16[1024,128]{1,0:T(8,128)(2,1)S(1)}, u32[]{:S(2)}, u32[]{:S(2)}) collective-permute-start(bf16[1024,128]{1,0:T(8,128)(2,1)} %bitcast.26), channel_id=1, source_target_pairs={{0,2},{2,4},{4,6},{6,8},{8,10},{10,12},{12,14},{14,16},{16,18},{18... | collective-permute-start | bytes 786440 | tf_op jit(solution)/shard_map/ppermute | solution.py:176
  6.9 1.9 collective-permute-start.1
  8.8 1.1 pad_maximum_fusion.1
  10.5 0.0 copy-done.3
  10.5 0.0 copy-done.2
  10.6 0.0 collective-permute-done.kb_ref
  10.6 2.7 %collective-permute-done.1.vb_ref = bf16[1024,128]{1,0:T(8,128)(2,1)S(1)} collective-permute-done((bf16[1024,128]{1,0:T(8,128)(2,1)}, bf16[1024,128]{1,0:T(8,128)(2,1)S(1)}, u32[]{:S(2)}, u32[]{:S(2)}) %collective-permute-start.1) | collective-permute-done | bytes 262176 | tf_op jit(solution)/shard_map/ppermute | solution.py:176
  13.3 0.0 copy-done
  13.3 0.0 copy-done.1
  13.3 3.2 %shard_map.84 = (f32[2,1024]{1,0:T(2,128)S(1)}, bf16[256,128]{1,0:T(8,128)(2,1)S(1)}) custom-call(s32[1]{0:T(128)} %bitcast.at, s32[1]{0:T(128)} %bitcast.25.route, bf16[1024,128]{1,0:T(8,128)(2,1)S(1)} %bitcast.37, bf16[1024,128]{1,0:T(8,128)(2,1)S(1)} %bitcast.40, bf16[1024,128]{1,0:T(8,128)(2,1)S(1)} %bitcast.28, bf16[1024,128]{1,0:T(8,128)(2,1)S(1)} %bitcast.33, ...), custom_call_target="tpu_custom_call" | custom-call | tf_op jit(solution)/shard_map/pallas_call | solution.py:196
  16.5 0.1 copy.17
  16.6 0.3 maximum_bitcast_fusion
  16.9 1.8 pad_maximum_fusion
  18.7 87.5 %all_to_all.10.x_ref = bf16[256,9,2,128]{3,2,1,0:T(2,128)(2,1)S(1)} all-to-all(bf16[256,9,2,128]{3,2,1,0:T(2,128)(2,1)S(1)} %pad_maximum_fusion), channel_id=1, replica_groups=mesh['seq'=256,'head'=2] {'seq'}, dimensions={0} | all-to-all | bytes 2359296 | tf_op jit(solution)/shard_map/all_to_all | solution.py:216
  106.2 4.8 %fusion.2 = s32[256]{0:T(256)S(1)} fusion(bf16[256,9,2,128]{3,2,1,0:T(2,128)(2,1)S(1)} %all_to_all.10.x_ref), kind=kLoop, calls=%fused_computation.8 | loop fusion | flops 256 | bytes 1536 | tf_op jit(solution)/shard_map/convert_element_type | solution.py:217
  111.0 0.5 shard_map.85
  111.5 1.3 shard_map.86
  112.8 71.5 %all_to_all.11 = bf16[256,9,2,128]{3,2,1,0:T(2,128)(2,1)S(1)} all-to-all(bf16[256,9,2,128]{3,2,1,0:T(2,128)(2,1)S(1)} %shard_map.86), channel_id=1, replica_groups=mesh['seq'=256,'head'=2] {'seq'}, dimensions={0} | all-to-all | bytes 2359296 | tf_op jit(solution)/shard_map/all_to_all | solution.py:221
  184.3 0.7 fusion.3
  185.0 10.3 %shard_map.87 = (bf16[1024,128]{1,0:T(8,128)(2,1)}, bf16[1024,128]{1,0:T(8,128)(2,1)}, f32[1024,128]{1,0:T(8,128)S(1)}, f32[1024,128]{1,0:T(8,128)S(1)}, bf16[10...) custom-call(s32[1]{0:T(128)} %bitcast.at, bf16[1024,128]{1,0:T(8,128)(2,1)S(1)} %bitcast.38, ...), custom_call_target="tpu_custom_call" | custom-call | tf_op jit(solution)/shard_map/pallas_call | solution.py:227
  195.3 1.9 collective-permute-start.2
  197.2 2.2 %collective-permute-start.3 = (bf16[1024,128]{1,0:T(8,128)(2,1)S(1)}, bf16[1024,128]{1,0:T(8,128)(2,1)S(1)}, u32[]{:S(2)}, u32[]{:S(2)}) collective-permute-start(bf16[1024,128]{1,0:T(8,128)(2,1)S(1)} %get-tuple-element.27), channel_id=1, source_target_pairs={{2,0},{4,2},{6,4},{8,6},{10,8},{12,10},{14,12},{16,14},{18,16},{20... | collective-permute-start | bytes 786440 | tf_op jit(solution)/shard_map/ppermute | solution.py:176
  199.4 0.1 slice.51
  199.5 5.1 %shard_map.88 = (f32[1024,128]{1,0:T(8,128)S(1)}, f32[1024,128]{1,0:T(8,128)S(1)}) custom-call(bf16[1024,128]{1,0:T(8,128)(2,1)S(1)} %bitcast.43, bf16[1024,128]{1,0:T(8,128)(2,1)S(1)} %bitcast.42, bf16[1024,128]{1,0:T(8,128)(2,1)S(1)} %bitcast.30, bf16[1024,128]{1,0:T(8,128)(2,1)S(1)} %bitcast.35, bf16[256,128]{1,0:T(8,128)(2,1)S(1)} %bitcast.46, ...), custom_call_target="tpu_custom_call" | custom-call | tf_op jit(solution)/shard_map/pallas_call | solution.py:236
  204.6 0.0 collective-permute-done.2
  204.6 0.8 fusion
  205.4 1.9 collective-permute-done.3
  207.3 0.8 fusion.1
  (2 shorter events, 0.0 us)
Async XLA Ops:
  0.6 12.6 %copy-start = (bf16[1,1024,128]{2,1,0:T(8,128)(2,1)S(1)}, bf16[1,1024,128]{2,1,0:T(8,128)(2,1)}, u32[]{:S(2)}) copy-start(bf16[1,1024,128]{2,1,0:T(8,128)(2,1)} %param.6) | copy-start | bytes 786436
  0.6 12.6 %copy-start.1 = (bf16[1,1024,128]{2,1,0:T(8,128)(2,1)S(1)}, bf16[1,1024,128]{2,1,0:T(8,128)(2,1)}, u32[]{:S(2)}) copy-start(bf16[1,1024,128]{2,1,0:T(8,128)(2,1)} %param.7) | copy-start | bytes 786436
  0.7 9.9 %copy-start.3 = (bf16[1,1024,128]{2,1,0:T(8,128)(2,1)S(1)}, bf16[1,1024,128]{2,1,0:T(8,128)(2,1)}, u32[]{:S(2)}) copy-start(bf16[1,1024,128]{2,1,0:T(8,128)(2,1)} %param.8) | copy-start | bytes 786436
  0.7 9.9 %copy-start.2 = (bf16[1,1024,128]{2,1,0:T(8,128)(2,1)S(1)}, bf16[1,1024,128]{2,1,0:T(8,128)(2,1)}, u32[]{:S(2)}) copy-start(bf16[1,1024,128]{2,1,0:T(8,128)(2,1)} %param.5) | copy-start | bytes 786436
  0.7 9.9 %collective-permute-start = (bf16[1024,128]{1,0:T(8,128)(2,1)}, bf16[1024,128]{1,0:T(8,128)(2,1)S(1)}, u32[]{:S(2)}, u32[]{:S(2)}) collective-permute-start(bf16[1024,128]{1,0:T(8,128)(2,1)} %bitcast.26), channel_id=1, source_target_pairs={{0,2},{2,4},{4,6},{6,8},{8,10},{10,12},{12,14},{14,16},{16,18},{18... | collective-permute-start | bytes 786440 | tf_op jit(solution)/shard_map/ppermute | solution.py:176
  6.9 6.4 %collective-permute-start.1 = (bf16[1024,128]{1,0:T(8,128)(2,1)}, bf16[1024,128]{1,0:T(8,128)(2,1)S(1)}, u32[]{:S(2)}, u32[]{:S(2)}) collective-permute-start(bf16[1024,128]{1,0:T(8,128)(2,1)} %bitcast.31), channel_id=1, source_target_pairs={{0,2},{2,4},{4,6},{6,8},{8,10},{10,12},{12,14},{14,16},{16,18},{18... | collective-permute-start | bytes 786440 | tf_op jit(solution)/shard_map/ppermute | solution.py:176
  195.3 9.3 %collective-permute-start.2 = (bf16[1024,128]{1,0:T(8,128)(2,1)S(1)}, bf16[1024,128]{1,0:T(8,128)(2,1)S(1)}, u32[]{:S(2)}, u32[]{:S(2)}) collective-permute-start(bf16[1024,128]{1,0:T(8,128)(2,1)S(1)} %get-tuple-element.25), channel_id=1, source_target_pairs={{2,0},{4,2},{6,4},{8,6},{10,8},{12,10},{14,12},{16,14},{18,16},{20... | collective-permute-start | bytes 786440 | tf_op jit(solution)/shard_map/ppermute | solution.py:176
  197.2 10.1 %collective-permute-start.3 = (bf16[1024,128]{1,0:T(8,128)(2,1)S(1)}, bf16[1024,128]{1,0:T(8,128)(2,1)S(1)}, u32[]{:S(2)}, u32[]{:S(2)}) collective-permute-start(bf16[1024,128]{1,0:T(8,128)(2,1)S(1)} %get-tuple-element.27), channel_id=1, source_target_pairs={{2,0},{4,2},{6,4},{8,6},{10,8},{12,10},{14,12},{16,14},{18,16},{20... | collective-permute-start | bytes 786440 | tf_op jit(solution)/shard_map/ppermute | solution.py:176

commit v2 on v1

v2 whole, which is shorter than its diff:
```python
import functools
import math

import jax
import jax.numpy as jnp
from jax import lax
from jax.experimental import pallas as pl
from jax.experimental.pallas import tpu as pltpu
from jax.sharding import PartitionSpec as P

F32 = jnp.float32
BF16 = jnp.bfloat16
NT = (((1,), (1,)), ((), ()))
NN = (((1,), (0,)), ((), ()))
CHUNK = 256
LONG = 1024
INF = float("inf")
VMEM_LIMIT = 32 * 1024 * 1024


def dot(a, b, dims=NN):
    return lax.dot_general(a, b, dims, preferred_element_type=F32)


def chunks(rows, size=CHUNK):
    return [slice(at, at + size) for at in range(0, rows, size)]


def causal(scores, first):
    kpos = lax.broadcasted_iota(jnp.int32, scores.shape, 0)
    qpos = lax.broadcasted_iota(jnp.int32, scores.shape, 1) + first
    return jnp.where(kpos <= qpos, scores, -INF)


def call(kernel, out_shape, n_in, scalars=0):
    vmem = pl.BlockSpec(memory_space=pltpu.VMEM)
    smem = pl.BlockSpec(memory_space=pltpu.SMEM)
    return pl.pallas_call(
        kernel,
        out_shape=out_shape,
        in_specs=[smem] * scalars + [vmem] * n_in,
        out_specs=jax.tree.map(lambda _: vmem, out_shape),
        compiler_params=pltpu.CompilerParams(vmem_limit_bytes=VMEM_LIMIT),
    )


def thirds(x):
    high = x.astype(BF16).astype(F32)
    middle = (x - high).astype(BF16).astype(F32)
    return high, middle, x - high - middle


def stats_kernel(
    scale, at, route, q_ref, g_ref, k_ref, v_ref, before_ref, own_pairs, swapped_pairs, q_pairs, g_pairs,
    out_ref, notes_ref, spread_ref, rows_ref, sems,
):
    leading = at[0] == 0
    half = own_pairs.shape[1]
    middle = q_pairs.shape[0]
    swap = route[0] & 1 == 1
    kv_to = spread_ref.at[:, :half]
    copies = [
        pltpu.make_async_copy(q_pairs, spread_ref.at[:middle, half : 2 * half], sems.at[0]),
        pltpu.make_async_copy(g_pairs, spread_ref.at[middle:, half : 2 * half], sems.at[1]),
    ]
    for copy in copies:
        copy.start()

    @pl.when(swap)
    def _():
        pltpu.make_async_copy(swapped_pairs, kv_to, sems.at[2]).start()

    @pl.when(jnp.logical_not(swap))
    def _():
        pltpu.make_async_copy(own_pairs, kv_to, sems.at[2]).start()

    rows = k_ref.shape[0]
    kb_ref, vb_ref = before_ref.at[:rows], before_ref.at[rows:]
    places = rows_ref.shape[1]
    parts = q_ref.shape[0] // places
    rows_ref[...] = jnp.full(rows_ref.shape, route[0].astype(F32))
    for cols in chunks(q_ref.shape[0]):
        q, g = q_ref[cols], g_ref[cols]
        own = causal(dot(k_ref[: cols.stop], q, NT) * scale, cols.start)
        before = dot(kb_ref[...], q, NT) * scale
        peak_before = jnp.where(leading, -INF, jnp.max(before, 0, keepdims=True))
        peak = jnp.maximum(jnp.max(own, 0, keepdims=True), peak_before)
        own = jnp.exp2(own - peak)
        before = jnp.exp2(before - jnp.where(leading, INF, peak))
        total = jnp.sum(own, 0, keepdims=True) + jnp.sum(before, 0, keepdims=True)
        pushed = jnp.sum(own * dot(v_ref[: cols.stop], g, NT), 0, keepdims=True)
        pushed += jnp.sum(before * dot(vb_ref[...], g, NT), 0, keepdims=True)
        for kind, row in enumerate((peak + jnp.log2(total), pushed / total)):
            out_ref[kind : kind + 1, cols] = row
            for i, third in enumerate(thirds(row)):
                for at_row in range(0, CHUNK, places):
                    to = (3 * kind + i) * parts + (cols.start + at_row) // places
                    rows_ref[to : to + 1] = third[:, at_row : at_row + places]
    notes_ref[...] = rows_ref[...].T.astype(BF16)
    for copy in copies:
        copy.wait()
    pltpu.make_async_copy(own_pairs, kv_to, sems.at[2]).wait()


def read_notes(notes_ref, count):
    rows = notes_ref[...].astype(F32).T
    parts = count // rows.shape[1]
    per = parts * LONG // count
    sums = [sum(rows[(3 * kind + i) * parts : (3 * kind + i + 1) * parts] for i in range(3)) for kind in range(2)]
    return [
        [jnp.concatenate([total[t : t + 1] for t in range(at, at + per)], 1) for at in range(0, parts, per)]
        for total in sums
    ]


def joined(elsewhere, scores):
    peak = jnp.max(scores, 0, keepdims=True)
    raw = jnp.exp2(scores - peak)
    here = peak + jnp.log2(jnp.sum(raw, 0, keepdims=True))
    top = jnp.maximum(elsewhere, here)
    log_total = top + jnp.log2(jnp.exp2(elsewhere - top) + jnp.exp2(here - top))
    return raw * jnp.exp2(peak - log_total), log_total, jnp.exp2(elsewhere - log_total)


def local_kernel(
    scale, at, q_ref, g_ref, k_ref, v_ref, before_ref, stats_ref,
    out_ref, shaped_keys_ref, keys_ref, so_ref, wo_ref, g_t_ref,
):
    leading = at[0] == 0
    rows = k_ref.shape[0]
    kb_ref, vb_ref = before_ref.at[:rows], before_ref.at[rows:]
    g_t_ref[...] = g_ref[...].T
    k_t, kb_t = k_ref[...].T, kb_ref[...].T
    v_t, vb_t = v_ref[...].T, vb_ref[...].T
    for cols in chunks(q_ref.shape[0]):
        q, g = q_ref[cols], g_ref[cols]
        keys = slice(0, cols.stop)
        total, drift = stats_ref[0:1, cols], stats_ref[1:2, cols]

        def shape(weights, v):
            return (weights.astype(F32) * (dot(v, g, NT) - drift)).astype(BF16)

        wo = jnp.exp2(causal(dot(k_ref[keys], q, NT) * scale, cols.start) - total).astype(BF16)
        so = shape(wo, v_ref[keys])
        wb = jnp.exp2(dot(kb_ref[...], q, NT) * scale - jnp.where(leading, INF, total)).astype(BF16)
        sb = shape(wb, vb_ref[...])
        out_ref[:, cols] = dot(v_t[:, keys], wo) + dot(vb_t, wb)
        shaped_keys_ref[:, cols] = dot(k_t[:, keys], so) + dot(kb_t, sb)
        keys_ref[:, cols] = dot(k_t[:, keys], wo) + dot(kb_t, wb)
        wo_ref[keys, cols] = wo
        so_ref[keys, cols] = so


def next_kernel(scale, qg_ref, k_ref, v_ref, stats_ref, s_ref, w_ref):
    rows = k_ref.shape[0]
    q_ref, g_ref = qg_ref.at[:rows], qg_ref.at[rows:]
    for cols in chunks(rows):
        weights = jnp.exp2(dot(k_ref[...], q_ref[cols], NT) * scale - stats_ref[0:1, cols]).astype(BF16)
        pushed = dot(v_ref[...], g_ref[cols], NT)
        w_ref[:, cols] = weights
        s_ref[:, cols] = (weights.astype(F32) * (pushed - stats_ref[1:2, cols])).astype(BF16)


def scaled(q, g, shares_ref):
    down = jnp.concatenate([shares_ref[...]] * 4, 0).T
    share, delta = down[:, 0:1], down[:, 1:2]
    q, g = q.astype(F32), g.astype(F32)
    return (q * share).astype(BF16), jnp.concatenate([(q * delta).astype(BF16), (g * share).astype(BF16)], 1)


def query_kernel(
    scale, factor, q_ref, g_ref, partner_ref, stats_ref, out_ref, shaped_keys_ref, keys_ref, g_t_ref,
    att_ref, dq_ref, shares_ref,
):
    rows = q_ref.shape[0]
    kp_ref, vp_ref = partner_ref.at[:rows], partner_ref.at[rows:]
    kp_t, vp_t = kp_ref[...].T, vp_ref[...].T
    for cols in chunks(rows, LONG):
        q, g = q_ref[cols], g_ref[cols]
        weights, _, share = joined(stats_ref[0:1, cols], dot(kp_ref[...], q, NT) * scale)
        weights = weights.astype(BF16)
        attended = (dot(vp_t, weights) + share * out_ref[:, cols]).astype(BF16).astype(F32)
        att_ref[cols] = attended.T.astype(BF16)
        drift = jnp.sum(attended * g_t_ref[:, cols].astype(F32), 0, keepdims=True)
        delta = share * (stats_ref[1:2, cols] - drift)
        shaped = (weights.astype(F32) * (dot(vp_ref[...], g, NT) - drift)).astype(BF16)
        dq = dot(kp_t, shaped) + share * shaped_keys_ref[:, cols] + delta * keys_ref[:, cols]
        dq_ref[cols] = (dq * factor).T.astype(BF16)
        shares_ref[0:1, cols] = share
        shares_ref[1:2, cols] = delta


def partner_terms_kernel(scale, factor, qg_ref, k_ref, v_ref, notes_ref, dk_ref, dv_ref, s_ref, w_ref):
    rows = k_ref.shape[0]
    q_ref, g_ref = qg_ref.at[:rows], qg_ref.at[rows:]
    elsewhere, pushed_there = read_notes(notes_ref, rows)
    for t, cols in enumerate(chunks(rows, LONG)):
        q, g = q_ref[cols], g_ref[cols]
        weights, _, share = joined(elsewhere[t], dot(k_ref[...], q, NT) * scale)
        pushed = dot(v_ref[...], g, NT)
        drift = share * pushed_there[t] + jnp.sum(weights * pushed, 0, keepdims=True)
        weights = weights.astype(BF16)
        s_ref[:, cols] = (weights.astype(F32) * (pushed - drift)).astype(BF16)
        w_ref[:, cols] = weights
    dk_ref[...] = (dot(s_ref[...], q_ref[...]) * factor).astype(BF16)
    dv_ref[...] = dot(w_ref[...], g_ref[...]).astype(BF16)


def sum_kernel(
    factor, q_ref, g_ref, qg_next_ref, shares_ref, shares_next_ref, so_ref, wo_ref, sn_ref, wn_ref, dkp_ref, dvp_ref,
    dk_ref, dv_ref, key_x, both_x, next_key_x, next_both_x,
):
    rows, width = q_ref.shape
    key_x[...], both_x[...] = scaled(q_ref[...], g_ref[...], shares_ref)
    next_key_x[...], next_both_x[...] = scaled(qg_next_ref[:rows], qg_next_ref[rows:], shares_next_ref)
    for keys in chunks(rows):
        later = slice(keys.start, rows)
        both = dot(wn_ref[keys], next_both_x[...])
        dk = (dot(sn_ref[keys], next_key_x[...]) + both[:, :width]) * factor
        dk = dk.astype(BF16).astype(F32) + dkp_ref[keys].astype(F32)
        dv = both[:, width:].astype(BF16).astype(F32) + dvp_ref[keys].astype(F32)
        both = dot(wo_ref[keys, later], both_x[later])
        dk_ref[keys] = (dk + (dot(so_ref[keys, later], key_x[later]) + both[:, :width]) * factor).astype(BF16)
        dv_ref[keys] = (dv + both[:, width:]).astype(BF16)


def partner_kernel(notes_ref, partner_ref, inverse_ref):
    n = partner_ref.shape[1]
    route = (notes_ref[...].astype(F32).T[-1:]).astype(jnp.int32) >> 1
    lane = lax.broadcasted_iota(jnp.int32, route.shape, 1)

    def section(holder, s):
        far = 1 << s
        across = jnp.where((lane >> s) & 1 == 1, pltpu.roll(holder, far, 1), pltpu.roll(holder, n - far, 1))
        return jnp.where((route >> s) & 1 == 1, across, holder)

    sections = range(n.bit_length() - 1)
    partner_ref[...] = functools.reduce(section, sections, lane)
    inverse_ref[...] = functools.reduce(section, reversed(sections), lane)


def reorder_kernel(partner_ref, inverse_ref, x_ref, out_ref):
    keep = x_ref.shape[1] // 2

    def body(d, carry):
        out_ref[d, :keep] = x_ref[partner_ref[0, d], :keep]
        out_ref[d, keep:] = x_ref[inverse_ref[0, d], keep:]
        return carry

    lax.fori_loop(0, x_ref.shape[0], body, 0, unroll=8)


def shifted(x, distance):
    n = lax.axis_size("seq")
    return lax.ppermute(x, "seq", [(i, i + distance) for i in range(n) if 0 <= i + distance < n])


def swapped(x):
    return lax.ppermute(x, "seq", [(i, i ^ 1) for i in range(lax.axis_size("seq"))])


def exchange(x):
    groups = [list(range(core, lax.axis_size("seq"), 2)) for core in range(2)]
    return lax.all_to_all(x, "seq", 0, 0, axis_index_groups=groups, tiled=True)


def local(queries, keys, values, out_grad, route):
    q, k, v, g = queries[0], keys[0], values[0], out_grad[0]
    rows, width = q.shape
    n = lax.axis_size("seq")
    me = lax.axis_index("seq")
    factor = width**-0.5
    scale = factor * math.log2(math.e)
    at = me.reshape(1)
    places = n // 2
    part = 2 * rows // places
    swap = (route[0, 0] & 1) == 1
    block = jax.ShapeDtypeStruct((rows, width), BF16)

    vmem = pl.BlockSpec(memory_space=pltpu.VMEM)
    smem = pl.BlockSpec(memory_space=pltpu.SMEM)
    params = pltpu.CompilerParams(vmem_limit_bytes=VMEM_LIMIT)

    kv_own = jnp.concatenate([k, v])
    kv_before = shifted(kv_own, 1)
    kv_swapped = swapped(kv_own)

    def pairs(x):
        return x.reshape(-1, part // 2, 2, width)

    anywhere = pl.BlockSpec(memory_space=pl.ANY)
    stats, notes, spread = pl.pallas_call(
        functools.partial(stats_kernel, scale),
        out_shape=(
            jax.ShapeDtypeStruct((2, rows), F32),
            jax.ShapeDtypeStruct((places, width), BF16),
            jax.ShapeDtypeStruct((places, part + 1, 2, width), BF16),
        ),
        in_specs=[smem] * 2 + [vmem] * 5 + [anywhere] * 4,
        out_specs=(vmem, vmem, anywhere),
        scratch_shapes=[pltpu.VMEM((width, places), F32), pltpu.SemaphoreType.DMA((3,))],
        compiler_params=params,
    )(at, route.reshape(1), q, g, k, v, kv_before, pairs(kv_own), pairs(kv_swapped), pairs(q), pairs(g))
    spread = spread.at[:, part].set(jnp.broadcast_to(notes[:, None], (places, 2, width)))
    spread = exchange(spread)
    square = jax.ShapeDtypeStruct((rows, rows), BF16)
    across32 = jax.ShapeDtypeStruct((width, rows), F32)
    from_local = pl.pallas_call(
        functools.partial(local_kernel, scale),
        out_shape=(across32,) * 3 + (square,) * 2 + (jax.ShapeDtypeStruct((width, rows), BF16),),
        in_specs=[smem] + [vmem] * 6,
        out_specs=(vmem,) * 6,
        compiler_params=params,
    )(at, q, g, k, v, kv_before, stats)
    qg_next, stats_next = shifted((jnp.concatenate([q, g]), stats), -1)
    spread, from_local, qg_next, stats_next = lax.optimization_barrier((spread, from_local, qg_next, stats_next))
    out, shaped_keys, weighted_keys, so, wo, g_t = from_local
    index = jax.ShapeDtypeStruct((1, places), jnp.int32)
    partner, inverse = call(partner_kernel, (index, index), 1)(spread[:, -1, 0])
    moved = call(reorder_kernel, jax.ShapeDtypeStruct(spread.shape, BF16), 1, 2)(partner, inverse, spread)
    moved = exchange(moved)
    from_next = pl.pallas_call(
        functools.partial(next_kernel, scale),
        out_shape=(square,) * 2,
        in_specs=[vmem] * 4,
        out_specs=(vmem,) * 2,
        compiler_params=params,
    )(qg_next, k, v, stats_next)
    moved, from_next = lax.optimization_barrier((moved, from_next))
    sn, wn = from_next
    kv = moved[:, : part // 2].reshape(2 * rows, width)
    rest = moved[:, part // 2 :]
    rest = jnp.where(swap, swapped(rest), rest)
    qg = rest[:, : part // 2].reshape(2 * rows, width)
    notes = rest[:, -1, 0]

    attended, query_grad, shares = pl.pallas_call(
        functools.partial(query_kernel, scale, factor),
        out_shape=(block, block, jax.ShapeDtypeStruct((2, rows), F32)),
        in_specs=[vmem] * 8,
        out_specs=(vmem,) * 3,
        compiler_params=params,
    )(q, g, kv, stats, out, shaped_keys, weighted_keys, g_t)
    shares_next = shifted(shares, -1)
    dk, dv = pl.pallas_call(
        functools.partial(partner_terms_kernel, scale, factor),
        out_shape=(block, block),
        in_specs=[vmem] * 4,
        out_specs=(vmem,) * 2,
        scratch_shapes=[pltpu.VMEM((rows, rows), BF16)] * 2,
        compiler_params=params,
    )(qg, k, v, notes)
    one, two = pltpu.VMEM((rows, width), BF16), pltpu.VMEM((rows, 2 * width), BF16)
    key_grad, value_grad = pl.pallas_call(
        functools.partial(sum_kernel, factor),
        out_shape=(block, block),
        in_specs=[vmem] * 11,
        out_specs=(vmem,) * 2,
        scratch_shapes=[one, two, one, two],
        compiler_params=params,
    )(q, g, qg_next, shares, shares_next, so, wo, sn, wn, dk, dv)
    return attended[None], query_grad[None], key_grad[None], value_grad[None]


def solution(mesh):
    whole = P("head", "seq", None)
    return jax.shard_map(
        local,
        mesh=mesh,
        in_specs=(whole,) * 4 + (P("head", "seq"),),
        out_specs=(whole,) * 4,
        check_vma=False,
    )
```

time: 208 us -> 190 us (0.913)
  the two profiles are of different devices: /device:TPU:1 before, /device:TPU:34 now
where the time goes in v2:
time: 190 us; the launch traced here: 189 us
  waiting for transfers between devices  101 us (53%)
  starting transfers between devices  50.2 us (26%)
  Pallas kernels  22.3 us (12%)
  local copies, waits for them, and re-layouts  12.6 us (7%)
    all_to_all x2, waiting for transfers between devices, exchange(): return lax.all_to_all(x, 'seq', 0, 0, axis_index_groups=groups, tiled=True)  59.5 us
    ppermute x4, waiting for transfers between devices, shifted(): lax.ppermute(x, 'seq', [(i, i + distance) for i in range(n) if 0 <= i + d...  41.5 us
    all_to_all x2, starting transfers between devices, exchange(): return lax.all_to_all(x, 'seq', 0, 0, axis_index_groups=groups, tiled=True)  24.6 us
    ppermute x4, starting transfers between devices, shifted(): lax.ppermute(x, 'seq', [(i, i + distance) for i in range(n) if 0 <= i + d...  14.1 us
    ppermute x2, starting transfers between devices, swapped(): lax.ppermute(x, 'seq', [(i, i ^ 1) for i in range(lax.axis_size('seq'))])  11.6 us
    unnamed x39, local copies, waits for them, and re-layouts  8.35 us
    pallas_call x1, Pallas kernels, local(): pl.pallas_call(functools.partial(query_kernel, scale, factor), out_shape=...  3.9 us
  transfers between devices with their start and end apart: 8, of which 4 were waited for; matrix products, arithmetic and copies ran while one was open for 1% of the time, Pallas kernels for 7%

profile of v2, /device:TPU:34, one launch (start us, length us, event | category | flops | bytes accessed | tf_op | source)
XLA Modules:
  0.0 189.1 jit_solution(13956731950333440686)
XLA Ops:
  0.6 0.0 copy-start.2
  0.6 0.0 copy-start.3
  0.7 0.0 copy-start
  0.7 0.0 copy-start.1
  0.7 1.1 pad_maximum_fusion
  1.8 1.9 %collective-permute-start = (bf16[2048,128]{1,0:T(8,128)(2,1)S(1)}, bf16[2048,128]{1,0:T(8,128)(2,1)S(1)}, u32[]{:S(2)}, u32[]{:S(2)}) collective-permute-start(bf16[2048,128]{1,0:T(8,128)(2,1)S(1)} %pad_maximum_fusion), channel_id=1, source_target_pairs={{0,2},{2,4},{4,6},{6,8},{8,10},{10,12},{12,14},{14,16},{16,18},{18... | collective-permute-start | bytes 1572872 | tf_op jit(solution)/shard_map/ppermute | solution.py:255
  3.7 4.1 %collective-permute-start.1 = (bf16[2048,128]{1,0:T(8,128)(2,1)S(1)}, bf16[2048,128]{1,0:T(8,128)(2,1)S(1)}, u32[]{:S(2)}, u32[]{:S(2)}) collective-permute-start(bf16[2048,128]{1,0:T(8,128)(2,1)S(1)} %pad_maximum_fusion), channel_id=1, source_target_pairs={{0,2},{2,0},{4,6},{6,4},{8,10},{10,8},{12,14},{14,12},{16,18},{18,... | collective-permute-start | bytes 1572872 | tf_op jit(solution)/shard_map/ppermute | solution.py:259
  8.5 8.3 %collective-permute-done.before_ref = bf16[2048,128]{1,0:T(8,128)(2,1)S(1)} collective-permute-done((bf16[2048,128]{1,0:T(8,128)(2,1)S(1)}, bf16[2048,128]{1,0:T(8,128)(2,1)S(1)}, u32[]{:S(2)}, u32[]{:S(2)}) %collective-permute-start) | collective-permute-done | bytes 524320 | tf_op jit(solution)/shard_map/ppermute | solution.py:255
  16.8 0.0 collective-permute-done.1
  16.8 0.0 copy-done.2
  16.8 0.0 copy-done.3
  16.8 0.0 copy-done
  16.9 0.0 copy-done.1
  16.9 3.8 %shard_map.84 = (f32[2,1024]{1,0:T(2,128)S(1)}, bf16[128,128]{1,0:T(8,128)(2,1)S(1)}, bf16[128,17,2,128]{3,2,1,0:T(2,128)(2,1)}) custom-call(s32[1]{0:T(128)} %bitcast.2.at, s32[1]{0:T(128)} %bitcast.22.route, bf16[1024,128]{1,0:T(8,128)(2,1)S(1)} %bitcast.23, bf16[1024,128]{1,0:T(8,128)(2,1)S(1)} %bitcast.29, bf16[1024,128]{1,0:T(8,128)(2,1)S(1)} %bitcast.36, ...), custom_call_target="tpu_custom_call" | custom-call | tf_op jit(solution)/shard_map/pallas_call | solution.py:292
  20.7 0.7 broadcast_dynamic-update-slice_fusion
  21.3 17.8 %all-to-all-start = ((bf16[128,17,2,128]{3,2,1,0:T(2,128)(2,1)}), bf16[128,17,2,128]{3,2,1,0:T(2,128)(2,1)S(1)}, u32[]{:S(2)}, u32[]{:S(2)}) async-start(bf16[128,17,2,128]{3,2,1,0:T(2,128)(2,1)} %broadcast_dynamic-update-slice_fusion), calls=%async_computation | async-start | bytes 2228224 | tf_op jit(solution)/shard_map/all_to_all | solution.py:264
  39.1 4.3 %collective-permute-start.2 = (bf16[2048,128]{1,0:T(8,128)(2,1)S(1)}, bf16[2048,128]{1,0:T(8,128)(2,1)S(1)}, u32[]{:S(2)}, u32[]{:S(2)}) collective-permute-start(bf16[2048,128]{1,0:T(8,128)(2,1)S(1)} %pad_maximum_fusion.1), channel_id=1, source_target_pairs={{2,0},{4,2},{6,4},{8,6},{10,8},{12,10},{14,12},{16,14},{18,16},{20... | collective-permute-start | bytes 1572872 | tf_op jit(solution)/shard_map/ppermute | solution.py:255
  43.4 4.8 %collective-permute-start.3 = (f32[2,1024]{1,0:T(2,128)S(1)}, f32[2,1024]{1,0:T(2,128)S(1)}, u32[]{:S(2)}, u32[]{:S(2)}) collective-permute-start(f32[2,1024]{1,0:T(2,128)S(1)} %get-tuple-element.50.stats_ref), channel_id=1, source_target_pairs={{2,0},{4,2},{6,4},{8,6},{10,8},{12,10},{14,12},{16,14},{18,16},{20... | collective-permute-start | bytes 24584 | tf_op jit(solution)/shard_map/ppermute | solution.py:255
  48.2 3.5 %shard_map.85 = (f32[128,1024]{1,0:T(8,128)S(1)}, f32[128,1024]{1,0:T(8,128)S(1)}, f32[128,1024]{1,0:T(8,128)S(1)}, bf16[1024,1024]{1,0:T(8,128)(2,1)S(1)}, bf16...) custom-call(s32[1]{0:T(128)} %bitcast.2.at, bf16[1024,128]{1,0:T(8,128)(2,1)S(1)} %bitcast.26, ...), custom_call_target="tpu_custom_call" | custom-call | tf_op jit(solution)/shard_map/pallas_call | solution.py:308
  51.6 0.0 copy-start.4
  51.6 1.3 copy-done.4
  53.0 0.0 copy-start.6
  53.0 1.3 copy-done.6
  54.3 0.8 copy-done.13
  55.1 0.8 copy-done.15
  55.9 0.8 copy-done.17
  56.7 33.2 %collective-permute-done.2.qg_ref.qg_next_ref = bf16[2048,128]{1,0:T(8,128)(2,1)S(1)} collective-permute-done((bf16[2048,128]{1,0:T(8,128)(2,1)S(1)}, bf16[2048,128]{1,0:T(8,128)(2,1)S(1)}, u32[]{:S(2)}, u32[]{:S(2)}) %collective-permute-start.2) | collective-permute-done | bytes 524320 | tf_op jit(solution)/shard_map/ppermute | solution.py:255
  90.0 0.8 copy-done.10
  90.8 0.0 collective-permute-done.3.stats_ref
  90.8 7.2 %all-to-all-done.x_ref = bf16[128,17,2,128]{3,2,1,0:T(2,128)(2,1)S(1)} async-done(((bf16[128,17,2,128]{3,2,1,0:T(2,128)(2,1)}), bf16[128,17,2,128]{3,2,1,0:T(2,128)(2,1)S(1)}, u32[]{:S(2)}, u32[]{:S(2)}) %all-to-all-start) | async-done | bytes 1114144 | tf_op jit(solution)/shard_map/all_to_all | solution.py:264
  98.0 0.5 shard_map.86
  98.5 2.0 %shard_map.87 = bf16[128,17,2,128]{3,2,1,0:T(2,128)(2,1)} custom-call(s32[1,128]{1,0:T(1,128)S(1)} %get-tuple-element.58.partner_ref, s32[1,128]{1,0:T(1,128)S(1)} %get-tuple-element.59.inverse_ref, bf16[128,17,2,128]{3,2,1,0:T(2,128)(2,1)S(1)} %all-to-all-done.x_ref), custom_call_target="tpu_custom_call" | custom-call | tf_op jit(solution)/shard_map/pallas_call | solution.py:320
  100.5 6.8 %all-to-all-start.1 = ((bf16[128,17,2,128]{3,2,1,0:T(2,128)(2,1)}), bf16[128,17,2,128]{3,2,1,0:T(2,128)(2,1)}, u32[]{:S(2)}, u32[]{:S(2)}) async-start(bf16[128,17,2,128]{3,2,1,0:T(2,128)(2,1)} %shard_map.87), calls=%async_computation.1 | async-start | bytes 2228224 | tf_op jit(solution)/shard_map/all_to_all | solution.py:264
  107.4 0.0 copy-start.11
  107.4 1.0 copy-done.11
  108.4 1.3 shard_map.88
  109.7 0.0 copy-start.8
  109.7 1.4 copy-done.8
  111.0 52.3 %all-to-all-done.1 = bf16[128,17,2,128]{3,2,1,0:T(2,128)(2,1)} async-done(((bf16[128,17,2,128]{3,2,1,0:T(2,128)(2,1)}), bf16[128,17,2,128]{3,2,1,0:T(2,128)(2,1)}, u32[]{:S(2)}, u32[]{:S(2)}) %all-to-all-start.1) | async-done | bytes 1114144 | tf_op jit(solution)/shard_map/all_to_all | solution.py:264
  163.4 1.5 copy.13
  164.9 0.0 copy-start.14
  164.9 0.0 copy-start.16
  164.9 0.0 copy-start.18
  165.0 7.4 %collective-permute-start.5 = (bf16[128,9,2,128]{3,0,2,1:T(8,128)(2,1)S(1)}, bf16[128,9,2,128]{3,0,2,1:T(8,128)(2,1)S(1)}, u32[]{:S(2)}, u32[]{:S(2)}) collective-permute-start(bf16[128,9,2,128]{3,0,2,1:T(8,128)(2,1)S(1)} %slice.45), channel_id=1, source_target_pairs={{0,2},{2,0},{4,6},{6,4},{8,10},{10,8},{12,14},{14,12},{16,18},{18,... | collective-permute-start | bytes 1769480 | tf_op jit(solution)/shard_map/ppermute | solution.py:259
  172.4 1.4 slice.41
  173.8 0.0 copy-done.14
  173.8 0.0 copy-done.16
  173.8 0.0 copy-done.18
  173.9 0.0 copy-start.9
  173.9 3.9 %shard_map.89 = (bf16[1024,128]{1,0:T(8,128)(2,1)}, bf16[1024,128]{1,0:T(8,128)(2,1)}, f32[2,1024]{1,0:T(2,128)S(1)}) custom-call(bf16[1024,128]{1,0:T(8,128)(2,1)S(1)} %bitcast.27, bf16[1024,128]{1,0:T(8,128)(2,1)S(1)} %bitcast.33, bf16[2048,128]{1,0:T(8,128)(2,1)S(1)} %bitcast.47, f32[2,1024]{1,0:T(2,128)S(1)} %get-tuple-element.50.stats_ref, ...), custom_call_target="tpu_custom_call" | custom-call | tf_op jit(solution)/shard_map/pallas_call | solution.py:337
  177.8 3.1 %collective-permute-start.4 = (f32[2,1024]{1,0:T(2,128)S(1)}, f32[2,1024]{1,0:T(2,128)S(1)}, u32[]{:S(2)}, u32[]{:S(2)}) collective-permute-start(f32[2,1024]{1,0:T(2,128)S(1)} %get-tuple-element.71.shares_ref), channel_id=1, source_target_pairs={{2,0},{4,2},{6,4},{8,6},{10,8},{12,10},{14,12},{16,14},{18,16},{20... | collective-permute-start | bytes 24584 | tf_op jit(solution)/shard_map/ppermute | solution.py:255
  180.9 0.0 collective-permute-done.5
  180.9 0.0 copy-start.7
  180.9 0.1 broadcast_select_fusion
  181.0 0.0 copy-start.12
  181.1 0.0 copy-start.5
  181.1 0.5 copy.14
  181.6 3.8 %shard_map.90 = (bf16[1024,128]{1,0:T(8,128)(2,1)S(1)}, bf16[1024,128]{1,0:T(8,128)(2,1)S(1)}) custom-call(bf16[2048,128]{1,0:T(8,128)(2,1)S(1)} %bitcast.45, bf16[1024,128]{1,0:T(8,128)(2,1)S(1)} %bitcast.39, bf16[1024,128]{1,0:T(8,128)(2,1)S(1)} %bitcast.44, bf16[128,128]{1,0:T(8,128)(2,1)S(1)} %slice_bitcast_fusion.notes_ref), custom_call_target="tpu_custom_call" | custom-call | tf_op jit(solution)/shard_map/pallas_call | solution.py:345
  185.4 0.0 collective-permute-done.4.shares_next_ref
  185.4 0.0 copy-done.9
  185.4 0.0 copy-done.7
  185.4 0.0 copy-done.12
  185.5 0.0 copy-done.5
  185.5 3.7 %shard_map.91 = (bf16[1024,128]{1,0:T(8,128)(2,1)}, bf16[1024,128]{1,0:T(8,128)(2,1)}) custom-call(bf16[1024,128]{1,0:T(8,128)(2,1)S(1)} %bitcast.28, bf16[1024,128]{1,0:T(8,128)(2,1)S(1)} %bitcast.34, bf16[2048,128]{1,0:T(8,128)(2,1)S(1)} %copy-done.12, f32[2,1024]{1,0:T(2,128)S(1)} %get-tuple-element.71.shares_ref, ...), custom_call_target="tpu_custom_call" | custom-call | tf_op jit(solution)/shard_map/pallas_call | solution.py:354
  (10 shorter events, 0.2 us)
Async XLA Ops:
  0.6 16.2 %copy-start.2 = (bf16[1,1024,128]{2,1,0:T(8,128)(2,1)S(1)}, bf16[1,1024,128]{2,1,0:T(8,128)(2,1)}, u32[]{:S(2)}) copy-start(bf16[1,1024,128]{2,1,0:T(8,128)(2,1)} %param.8) | copy-start | bytes 786436
  0.6 16.2 %copy-start.3 = (bf16[1,1024,128]{2,1,0:T(8,128)(2,1)S(1)}, bf16[1,1024,128]{2,1,0:T(8,128)(2,1)}, u32[]{:S(2)}) copy-start(bf16[1,1024,128]{2,1,0:T(8,128)(2,1)} %param.9) | copy-start | bytes 786436
  0.7 16.2 %copy-start = (bf16[1,1024,128]{2,1,0:T(8,128)(2,1)S(1)}, bf16[1,1024,128]{2,1,0:T(8,128)(2,1)}, u32[]{:S(2)}) copy-start(bf16[1,1024,128]{2,1,0:T(8,128)(2,1)} %param.7) | copy-start | bytes 786436
  0.7 16.2 %copy-start.1 = (bf16[1,1024,128]{2,1,0:T(8,128)(2,1)S(1)}, bf16[1,1024,128]{2,1,0:T(8,128)(2,1)}, u32[]{:S(2)}) copy-start(bf16[1,1024,128]{2,1,0:T(8,128)(2,1)} %param.10) | copy-start | bytes 786436
  1.8 15.0 %collective-permute-start = (bf16[2048,128]{1,0:T(8,128)(2,1)S(1)}, bf16[2048,128]{1,0:T(8,128)(2,1)S(1)}, u32[]{:S(2)}, u32[]{:S(2)}) collective-permute-start(bf16[2048,128]{1,0:T(8,128)(2,1)S(1)} %pad_maximum_fusion), channel_id=1, source_target_pairs={{0,2},{2,4},{4,6},{6,8},{8,10},{10,12},{12,14},{14,16},{16,18},{18... | collective-permute-start | bytes 1572872 | tf_op jit(solution)/shard_map/ppermute | solution.py:255
  3.7 13.1 %collective-permute-start.1 = (bf16[2048,128]{1,0:T(8,128)(2,1)S(1)}, bf16[2048,128]{1,0:T(8,128)(2,1)S(1)}, u32[]{:S(2)}, u32[]{:S(2)}) collective-permute-start(bf16[2048,128]{1,0:T(8,128)(2,1)S(1)} %pad_maximum_fusion), channel_id=1, source_target_pairs={{0,2},{2,0},{4,6},{6,4},{8,10},{10,8},{12,14},{14,12},{16,18},{18,... | collective-permute-start | bytes 1572872 | tf_op jit(solution)/shard_map/ppermute | solution.py:259
  21.3 76.6 %all-to-all-start = ((bf16[128,17,2,128]{3,2,1,0:T(2,128)(2,1)}), bf16[128,17,2,128]{3,2,1,0:T(2,128)(2,1)S(1)}, u32[]{:S(2)}, u32[]{:S(2)}) async-start(bf16[128,17,2,128]{3,2,1,0:T(2,128)(2,1)} %broadcast_dynamic-update-slice_fusion), calls=%async_computation | async-start | bytes 2228224 | tf_op jit(solution)/shard_map/all_to_all | solution.py:264
  39.1 50.8 %collective-permute-start.2 = (bf16[2048,128]{1,0:T(8,128)(2,1)S(1)}, bf16[2048,128]{1,0:T(8,128)(2,1)S(1)}, u32[]{:S(2)}, u32[]{:S(2)}) collective-permute-start(bf16[2048,128]{1,0:T(8,128)(2,1)S(1)} %pad_maximum_fusion.1), channel_id=1, source_target_pairs={{2,0},{4,2},{6,4},{8,6},{10,8},{12,10},{14,12},{16,14},{18,16},{20... | collective-permute-start | bytes 1572872 | tf_op jit(solution)/shard_map/ppermute | solution.py:255
  43.4 47.4 %collective-permute-start.3 = (f32[2,1024]{1,0:T(2,128)S(1)}, f32[2,1024]{1,0:T(2,128)S(1)}, u32[]{:S(2)}, u32[]{:S(2)}) collective-permute-start(f32[2,1024]{1,0:T(2,128)S(1)} %get-tuple-element.50.stats_ref), channel_id=1, source_target_pairs={{2,0},{4,2},{6,4},{8,6},{10,8},{12,10},{14,12},{16,14},{18,16},{20... | collective-permute-start | bytes 24584 | tf_op jit(solution)/shard_map/ppermute | solution.py:255
  51.6 1.3 copy-start.4
  53.0 1.3 copy-start.6
  54.3 0.8 copy-start.13
  55.1 0.8 copy-start.15
  55.9 0.8 copy-start.17
  90.0 0.8 copy-start.10
  100.5 62.8 %all-to-all-start.1 = ((bf16[128,17,2,128]{3,2,1,0:T(2,128)(2,1)}), bf16[128,17,2,128]{3,2,1,0:T(2,128)(2,1)}, u32[]{:S(2)}, u32[]{:S(2)}) async-start(bf16[128,17,2,128]{3,2,1,0:T(2,128)(2,1)} %shard_map.87), calls=%async_computation.1 | async-start | bytes 2228224 | tf_op jit(solution)/shard_map/all_to_all | solution.py:264
  107.4 1.0 copy-start.11
  109.7 1.4 copy-start.8
  164.9 9.0 %copy-start.14 = (f32[128,1024]{1,0:T(8,128)S(1)}, f32[128,1024]{1,0:T(8,128)}, u32[]{:S(2)}) copy-start(f32[128,1024]{1,0:T(8,128)} %copy-done.13) | copy-start | bytes 1572868
  164.9 9.0 %copy-start.16 = (f32[128,1024]{1,0:T(8,128)S(1)}, f32[128,1024]{1,0:T(8,128)}, u32[]{:S(2)}) copy-start(f32[128,1024]{1,0:T(8,128)} %copy-done.15) | copy-start | bytes 1572868
  164.9 9.0 %copy-start.18 = (f32[128,1024]{1,0:T(8,128)S(1)}, f32[128,1024]{1,0:T(8,128)}, u32[]{:S(2)}) copy-start(f32[128,1024]{1,0:T(8,128)} %copy-done.17) | copy-start | bytes 1572868
  165.0 16.0 %collective-permute-start.5 = (bf16[128,9,2,128]{3,0,2,1:T(8,128)(2,1)S(1)}, bf16[128,9,2,128]{3,0,2,1:T(8,128)(2,1)S(1)}, u32[]{:S(2)}, u32[]{:S(2)}) collective-permute-start(bf16[128,9,2,128]{3,0,2,1:T(8,128)(2,1)S(1)} %slice.45), channel_id=1, source_target_pairs={{0,2},{2,0},{4,6},{6,4},{8,10},{10,8},{12,14},{14,12},{16,18},{18,... | collective-permute-start | bytes 1769480 | tf_op jit(solution)/shard_map/ppermute | solution.py:259
  173.9 11.6 %copy-start.9 = (bf16[1024,1024]{1,0:T(8,128)(2,1)S(1)}, bf16[1024,1024]{1,0:T(8,128)(2,1)}, u32[]{:S(2)}) copy-start(bf16[1024,1024]{1,0:T(8,128)(2,1)} %copy-done.8) | copy-start | bytes 6291460
  177.8 7.7 %collective-permute-start.4 = (f32[2,1024]{1,0:T(2,128)S(1)}, f32[2,1024]{1,0:T(2,128)S(1)}, u32[]{:S(2)}, u32[]{:S(2)}) collective-permute-start(f32[2,1024]{1,0:T(2,128)S(1)} %get-tuple-element.71.shares_ref), channel_id=1, source_target_pairs={{2,0},{4,2},{6,4},{8,6},{10,8},{12,10},{14,12},{16,14},{18,16},{20... | collective-permute-start | bytes 24584 | tf_op jit(solution)/shard_map/ppermute | solution.py:255
  180.9 4.5 %copy-start.7 = (bf16[1024,1024]{1,0:T(8,128)(2,1)S(1)}, bf16[1024,1024]{1,0:T(8,128)(2,1)}, u32[]{:S(2)}) copy-start(bf16[1024,1024]{1,0:T(8,128)(2,1)} %copy-done.6) | copy-start | bytes 6291460
  181.0 4.4 %copy-start.12 = (bf16[2048,128]{1,0:T(8,128)(2,1)S(1)}, bf16[2048,128]{1,0:T(8,128)(2,1)}, u32[]{:S(2)}) copy-start(bf16[2048,128]{1,0:T(8,128)(2,1)} %copy-done.10) | copy-start | bytes 1572868
  181.1 4.4 %copy-start.5 = (bf16[1024,1024]{1,0:T(8,128)(2,1)S(1)}, bf16[1024,1024]{1,0:T(8,128)(2,1)}, u32[]{:S(2)}) copy-start(bf16[1024,1024]{1,0:T(8,128)(2,1)} %copy-done.4) | copy-start | bytes 6291460

commit v3 on v2

--- a/solution.py
+++ b/solution.py
@@ -5,6 +5,7 @@
 import jax.numpy as jnp
 from jax import lax
 from jax.experimental import pallas as pl
+from jax.experimental.layout import Layout, with_layout_constraint
 from jax.experimental.pallas import tpu as pltpu
 from jax.sharding import PartitionSpec as P
 
@@ -13,9 +14,10 @@
 NT = (((1,), (1,)), ((), ()))
 NN = (((1,), (0,)), ((), ()))
 CHUNK = 256
+MIDDLE = 512
 LONG = 1024
 INF = float("inf")
-VMEM_LIMIT = 32 * 1024 * 1024
+VMEM_LIMIT = 16 * 1024 * 1024
 
 
 def dot(a, b, dims=NN):
@@ -50,8 +52,19 @@
     return high, middle, x - high - middle
 
 
+def own_kernel(scale, q_ref, g_ref, k_ref, v_ref, out_ref):
+    for cols in chunks(q_ref.shape[0]):
+        q, g = q_ref[cols], g_ref[cols]
+        own = causal(dot(k_ref[: cols.stop], q, NT) * scale, cols.start)
+        peak = jnp.max(own, 0, keepdims=True)
+        own = jnp.exp2(own - peak)
+        out_ref[0:1, cols] = peak
+        out_ref[1:2, cols] = jnp.sum(own, 0, keepdims=True)
+        out_ref[2:3, cols] = jnp.sum(own * dot(v_ref[: cols.stop], g, NT), 0, keepdims=True)
+
+
 def stats_kernel(
-    scale, at, route, q_ref, g_ref, k_ref, v_ref, before_ref, own_pairs, swapped_pairs, q_pairs, g_pairs,
+    scale, at, route, q_ref, g_ref, own_ref, before_ref, own_pairs, swapped_pairs, q_pairs, g_pairs,
     out_ref, notes_ref, spread_ref, rows_ref, sems,
 ):
     leading = at[0] == 0
@@ -74,26 +87,24 @@
     def _():
         pltpu.make_async_copy(own_pairs, kv_to, sems.at[2]).start()
 
-    rows = k_ref.shape[0]
+    rows = q_ref.shape[0]
     kb_ref, vb_ref = before_ref.at[:rows], before_ref.at[rows:]
     places = rows_ref.shape[1]
     parts = q_ref.shape[0] // places
     rows_ref[...] = jnp.full(rows_ref.shape, route[0].astype(F32))
-    for cols in chunks(q_ref.shape[0]):
+    for cols in chunks(rows, MIDDLE):
         q, g = q_ref[cols], g_ref[cols]
-        own = causal(dot(k_ref[: cols.stop], q, NT) * scale, cols.start)
         before = dot(kb_ref[...], q, NT) * scale
-        peak_before = jnp.where(leading, -INF, jnp.max(before, 0, keepdims=True))
-        peak = jnp.maximum(jnp.max(own, 0, keepdims=True), peak_before)
-        own = jnp.exp2(own - peak)
+        peak_own = own_ref[0:1, cols]
+        peak = jnp.maximum(peak_own, jnp.where(leading, -INF, jnp.max(before, 0, keepdims=True)))
         before = jnp.exp2(before - jnp.where(leading, INF, peak))
-        total = jnp.sum(own, 0, keepdims=True) + jnp.sum(before, 0, keepdims=True)
-        pushed = jnp.sum(own * dot(v_ref[: cols.stop], g, NT), 0, keepdims=True)
-        pushed += jnp.sum(before * dot(vb_ref[...], g, NT), 0, keepdims=True)
+        share = jnp.exp2(peak_own - peak)
+        total = share * own_ref[1:2, cols] + jnp.sum(before, 0, keepdims=True)
+        pushed = share * own_ref[2:3, cols] + jnp.sum(before * dot(vb_ref[...], g, NT), 0, keepdims=True)
         for kind, row in enumerate((peak + jnp.log2(total), pushed / total)):
             out_ref[kind : kind + 1, cols] = row
             for i, third in enumerate(thirds(row)):
-                for at_row in range(0, CHUNK, places):
+                for at_row in range(0, MIDDLE, places):
                     to = (3 * kind + i) * parts + (cols.start + at_row) // places
                     rows_ref[to : to + 1] = third[:, at_row : at_row + places]
     notes_ref[...] = rows_ref[...].T.astype(BF16)
@@ -250,6 +261,18 @@
     lax.fori_loop(0, x_ref.shape[0], body, 0, unroll=8)
 
 
+def split_kernel(x_ref, first_ref, rest_ref, sems):
+    keep = first_ref.shape[1]
+    copies = [
+        pltpu.make_async_copy(x_ref.at[:, keep:], rest_ref, sems.at[0]),
+        pltpu.make_async_copy(x_ref.at[:, :keep], first_ref, sems.at[1]),
+    ]
+    for copy in copies:
+        copy.start()
+    for copy in copies:
+        copy.wait()
+
+
 def shifted(x, distance):
     n = lax.axis_size("seq")
     return lax.ppermute(x, "seq", [(i, i + distance) for i in range(n) if 0 <= i + distance < n])
@@ -262,6 +285,10 @@
 def exchange(x):
     groups = [list(range(core, lax.axis_size("seq"), 2)) for core in range(2)]
     return lax.all_to_all(x, "seq", 0, 0, axis_index_groups=groups, tiled=True)
+
+
+def rows_last(x):
+    return with_layout_constraint(x, Layout(tuple(range(x.ndim))))
 
 
 def local(queries, keys, values, out_grad, route):
@@ -289,6 +316,13 @@
         return x.reshape(-1, part // 2, 2, width)
 
     anywhere = pl.BlockSpec(memory_space=pl.ANY)
+    own_stats = pl.pallas_call(
+        functools.partial(own_kernel, scale),
+        out_shape=jax.ShapeDtypeStruct((3, rows), F32),
+        in_specs=[vmem] * 4,
+        out_specs=vmem,
+        compiler_params=params,
+    )(q, g, k, v)
     stats, notes, spread = pl.pallas_call(
         functools.partial(stats_kernel, scale),
         out_shape=(
@@ -296,11 +330,11 @@
             jax.ShapeDtypeStruct((places, width), BF16),
             jax.ShapeDtypeStruct((places, part + 1, 2, width), BF16),
         ),
-        in_specs=[smem] * 2 + [vmem] * 5 + [anywhere] * 4,
+        in_specs=[smem] * 2 + [vmem] * 4 + [anywhere] * 4,
         out_specs=(vmem, vmem, anywhere),
         scratch_shapes=[pltpu.VMEM((width, places), F32), pltpu.SemaphoreType.DMA((3,))],
         compiler_params=params,
-    )(at, route.reshape(1), q, g, k, v, kv_before, pairs(kv_own), pairs(kv_swapped), pairs(q), pairs(g))
+    )(at, route.reshape(1), q, g, own_stats, kv_before, pairs(kv_own), pairs(kv_swapped), pairs(q), pairs(g))
     spread = spread.at[:, part].set(jnp.broadcast_to(notes[:, None], (places, 2, width)))
     spread = exchange(spread)
     square = jax.ShapeDtypeStruct((rows, rows), BF16)
@@ -328,9 +362,19 @@
     )(qg_next, k, v, stats_next)
     moved, from_next = lax.optimization_barrier((moved, from_next))
     sn, wn = from_next
-    kv = moved[:, : part // 2].reshape(2 * rows, width)
-    rest = moved[:, part // 2 :]
-    rest = jnp.where(swap, swapped(rest), rest)
+    kv, rest = pl.pallas_call(
+        split_kernel,
+        out_shape=(
+            jax.ShapeDtypeStruct((places, part // 2, 2, width), BF16),
+            jax.ShapeDtypeStruct((places, part // 2 + 1, 2, width), BF16),
+        ),
+        in_specs=[anywhere],
+        out_specs=(vmem, vmem),
+        scratch_shapes=[pltpu.SemaphoreType.DMA((2,))],
+        compiler_params=params,
+    )(moved)
+    kv = kv.reshape(2 * rows, width)
+    rest = rows_last(jnp.where(swap, swapped(rest), rest))
     qg = rest[:, : part // 2].reshape(2 * rows, width)
     notes = rest[:, -1, 0]
 

time: 190 us -> 189 us (level)
  the two profiles are of different devices: /device:TPU:34 before, /device:TPU:1 now
where the time goes in v3:
time: 189 us; the launch traced here: 185 us
  waiting for transfers between devices  86.6 us (46%)
  starting transfers between devices  62.3 us (33%)
  Pallas kernels  22.1 us (12%)
  local copies, waits for them, and re-layouts  10.6 us (6%)
    all_to_all x2, waiting for transfers between devices, exchange(): return lax.all_to_all(x, 'seq', 0, 0, axis_index_groups=groups, tiled=True)  81.4 us
    all_to_all x2, starting transfers between devices, exchange(): return lax.all_to_all(x, 'seq', 0, 0, axis_index_groups=groups, tiled=True)  39.9 us
    ppermute x4, starting transfers between devices, shifted(): lax.ppermute(x, 'seq', [(i, i + distance) for i in range(n) if 0 <= i + d...  11.6 us
    ppermute x2, starting transfers between devices, swapped(): lax.ppermute(x, 'seq', [(i, i ^ 1) for i in range(lax.axis_size('seq'))])  10.8 us
    unnamed x38, local copies, waits for them, and re-layouts  9.46 us
    ppermute x4, waiting for transfers between devices, shifted(): lax.ppermute(x, 'seq', [(i, i + distance) for i in range(n) if 0 <= i + d...  5.2 us
    pallas_call x1, Pallas kernels, local(): pl.pallas_call(functools.partial(query_kernel, scale, factor), out_shape=...  3.92 us
  transfers between devices with their start and end apart: 8, of which 5 were waited for; matrix products, arithmetic and copies ran while one was open for 1% of the time, Pallas kernels for 7%

profile of v3, /device:TPU:1, one launch (start us, length us, event | category | flops | bytes accessed | tf_op | source)
XLA Modules:
  0.0 185.0 jit_solution(11694825791175043764)
XLA Ops:
  0.6 0.0 copy-start.3
  0.6 0.0 copy-start.2
  0.7 0.0 copy-start.1
  0.7 0.0 copy-start
  0.7 1.1 pad_maximum_fusion
  1.8 8.8 %collective-permute-start.1 = (bf16[2048,128]{1,0:T(8,128)(2,1)S(1)}, bf16[2048,128]{1,0:T(8,128)(2,1)S(1)}, u32[]{:S(2)}, u32[]{:S(2)}) collective-permute-start(bf16[2048,128]{1,0:T(8,128)(2,1)S(1)} %pad_maximum_fusion), channel_id=1, source_target_pairs={{0,2},{2,0},{4,6},{6,4},{8,10},{10,8},{12,14},{14,12},{16,18},{18,... | collective-permute-start | bytes 1572872 | tf_op jit(solution)/shard_map/ppermute | solution.py:282
  10.6 1.9 %collective-permute-start = (bf16[2048,128]{1,0:T(8,128)(2,1)S(1)}, bf16[2048,128]{1,0:T(8,128)(2,1)S(1)}, u32[]{:S(2)}, u32[]{:S(2)}) collective-permute-start(bf16[2048,128]{1,0:T(8,128)(2,1)S(1)} %pad_maximum_fusion), channel_id=1, source_target_pairs={{0,2},{2,4},{4,6},{6,8},{8,10},{10,12},{12,14},{14,16},{16,18},{18... | collective-permute-start | bytes 1572872 | tf_op jit(solution)/shard_map/ppermute | solution.py:278
  13.2 0.0 copy-done.3
  13.2 0.0 copy-done.2
  13.2 0.0 copy-done.1
  13.2 0.0 copy-done
  13.2 1.2 shard_map.84.own_ref
  14.4 0.0 collective-permute-done.1
  14.4 4.2 %collective-permute-done.before_ref = bf16[2048,128]{1,0:T(8,128)(2,1)S(1)} collective-permute-done((bf16[2048,128]{1,0:T(8,128)(2,1)S(1)}, bf16[2048,128]{1,0:T(8,128)(2,1)S(1)}, u32[]{:S(2)}, u32[]{:S(2)}) %collective-permute-start) | collective-permute-done | bytes 524320 | tf_op jit(solution)/shard_map/ppermute | solution.py:278
  18.6 2.3 %shard_map.85 = (f32[2,1024]{1,0:T(2,128)S(1)}, bf16[128,128]{1,0:T(8,128)(2,1)S(1)}, bf16[128,17,2,128]{3,2,1,0:T(2,128)(2,1)}) custom-call(s32[1]{0:T(128)} %bitcast.2.at, s32[1]{0:T(128)} %bitcast.23.route, bf16[1024,128]{1,0:T(8,128)(2,1)S(1)} %bitcast.25, bf16[1024,128]{1,0:T(8,128)(2,1)S(1)} %bitcast.32, f32[3,1024]{1,0:T(4,128)S(1)} %shard_map.84.own_ref, ...), custom_call_target="tpu_custom_call" | custom-call | tf_op jit(solution)/shard_map/pallas_call | solution.py:326
  21.0 0.7 broadcast_dynamic-update-slice_fusion
  21.6 17.6 %all-to-all-start = ((bf16[128,17,2,128]{3,2,1,0:T(2,128)(2,1)}), bf16[128,17,2,128]{3,2,1,0:T(2,128)(2,1)S(1)}, u32[]{:S(2)}, u32[]{:S(2)}) async-start(bf16[128,17,2,128]{3,2,1,0:T(2,128)(2,1)} %broadcast_dynamic-update-slice_fusion), calls=%async_computation | async-start | bytes 2228224 | tf_op jit(solution)/shard_map/all_to_all | solution.py:287
  39.3 5.3 %collective-permute-start.2 = (bf16[2048,128]{1,0:T(8,128)(2,1)S(1)}, bf16[2048,128]{1,0:T(8,128)(2,1)S(1)}, u32[]{:S(2)}, u32[]{:S(2)}) collective-permute-start(bf16[2048,128]{1,0:T(8,128)(2,1)S(1)} %pad_maximum_fusion.1), channel_id=1, source_target_pairs={{2,0},{4,2},{6,4},{8,6},{10,8},{12,10},{14,12},{16,14},{18,16},{20... | collective-permute-start | bytes 1572872 | tf_op jit(solution)/shard_map/ppermute | solution.py:278
  44.6 1.9 %collective-permute-start.3 = (f32[2,1024]{1,0:T(2,128)S(1)}, f32[2,1024]{1,0:T(2,128)S(1)}, u32[]{:S(2)}, u32[]{:S(2)}) collective-permute-start(f32[2,1024]{1,0:T(2,128)S(1)} %get-tuple-element.52.stats_ref), channel_id=1, source_target_pairs={{2,0},{4,2},{6,4},{8,6},{10,8},{12,10},{14,12},{16,14},{18,16},{20... | collective-permute-start | bytes 24584 | tf_op jit(solution)/shard_map/ppermute | solution.py:278
  46.6 3.5 %shard_map.86 = (f32[128,1024]{1,0:T(8,128)S(1)}, f32[128,1024]{1,0:T(8,128)S(1)}, f32[128,1024]{1,0:T(8,128)S(1)}, bf16[1024,1024]{1,0:T(8,128)(2,1)S(1)}, bf16...) custom-call(s32[1]{0:T(128)} %bitcast.2.at, bf16[1024,128]{1,0:T(8,128)(2,1)S(1)} %bitcast.28, ...), custom_call_target="tpu_custom_call" | custom-call | tf_op jit(solution)/shard_map/pallas_call | solution.py:342
  50.0 0.0 copy-start.4
  50.0 1.3 copy-done.4
  51.4 0.0 copy-start.6
  51.4 1.3 copy-done.6
  52.7 0.0 copy-start.12
  52.7 0.8 copy-done.12
  53.5 0.0 copy-start.14
  53.5 0.8 copy-done.14
  54.3 0.0 copy-start.16
  54.3 0.8 copy-done.16
  55.1 0.7 collective-permute-done.2.qg_ref.qg_next_ref
  55.8 0.2 collective-permute-done.3.stats_ref
  56.1 32.9 %all-to-all-done.x_ref = bf16[128,17,2,128]{3,2,1,0:T(2,128)(2,1)S(1)} async-done(((bf16[128,17,2,128]{3,2,1,0:T(2,128)(2,1)}), bf16[128,17,2,128]{3,2,1,0:T(2,128)(2,1)S(1)}, u32[]{:S(2)}, u32[]{:S(2)}) %all-to-all-start) | async-done | bytes 1114144 | tf_op jit(solution)/shard_map/all_to_all | solution.py:287
  89.0 0.5 shard_map.87
  89.5 1.9 %shard_map.88 = bf16[128,17,2,128]{3,2,1,0:T(2,128)(2,1)} custom-call(s32[1,128]{1,0:T(1,128)S(1)} %get-tuple-element.60.partner_ref, s32[1,128]{1,0:T(1,128)S(1)} %get-tuple-element.61.inverse_ref, bf16[128,17,2,128]{3,2,1,0:T(2,128)(2,1)S(1)} %all-to-all-done.x_ref), custom_call_target="tpu_custom_call" | custom-call | tf_op jit(solution)/shard_map/pallas_call | solution.py:354
  91.4 22.3 %all-to-all-start.1 = ((bf16[128,17,2,128]{3,2,1,0:T(2,128)(2,1)}), bf16[128,17,2,128]{3,2,1,0:T(2,128)(2,1)S(1)}, u32[]{:S(2)}, u32[]{:S(2)}) async-start(bf16[128,17,2,128]{3,2,1,0:T(2,128)(2,1)} %shard_map.88), calls=%async_computation.1 | async-start | bytes 2228224 | tf_op jit(solution)/shard_map/all_to_all | solution.py:287
  113.7 0.0 copy-start.13
  113.7 1.3 shard_map.89
  115.0 0.0 copy-start.8
  115.0 1.4 copy-done.8
  116.4 0.0 copy-start.10
  116.4 1.4 copy-done.10
  117.8 48.5 %all-to-all-done.1.x_ref = bf16[128,17,2,128]{3,2,1,0:T(2,128)(2,1)S(1)} async-done(((bf16[128,17,2,128]{3,2,1,0:T(2,128)(2,1)}), bf16[128,17,2,128]{3,2,1,0:T(2,128)(2,1)S(1)}, u32[]{:S(2)}, u32[]{:S(2)}) %all-to-all-start.1) | async-done | bytes 1114144 | tf_op jit(solution)/shard_map/all_to_all | solution.py:287
  166.3 0.1 shard_map.90
  166.4 2.1 %collective-permute-start.5 = (bf16[128,9,2,128]{3,2,1,0:T(2,128)(2,1)S(1)}, bf16[128,9,2,128]{3,2,1,0:T(2,128)(2,1)S(1)}, u32[]{:S(2)}, u32[]{:S(2)}) collective-permute-start(bf16[128,9,2,128]{3,2,1,0:T(2,128)(2,1)S(1)} %get-tuple-element.79), channel_id=1, source_target_pairs={{0,2},{2,0},{4,6},{6,4},{8,10},{10,8},{12,14},{14,12},{16,18},{18,... | collective-permute-start | bytes 1769480 | tf_op jit(solution)/shard_map/ppermute | solution.py:282
  168.5 0.0 copy-done.13
  168.5 0.0 copy-done.15
  168.5 0.0 copy-done.17
  168.5 0.0 copy-start.7
  168.5 0.0 copy-start.9
  168.5 3.9 %shard_map.91 = (bf16[1024,128]{1,0:T(8,128)(2,1)}, bf16[1024,128]{1,0:T(8,128)(2,1)}, f32[2,1024]{1,0:T(2,128)S(1)}) custom-call(bf16[1024,128]{1,0:T(8,128)(2,1)S(1)} %bitcast.29, bf16[1024,128]{1,0:T(8,128)(2,1)S(1)} %bitcast.36, bf16[2048,128]{1,0:T(8,128)(2,1)S(1)} %bitcast.51, f32[2,1024]{1,0:T(2,128)S(1)} %get-tuple-element.52.stats_ref, ...), custom_call_target="tpu_custom_call" | custom-call | tf_op jit(solution)/shard_map/pallas_call | solution.py:381
  172.4 2.4 %collective-permute-start.4 = (f32[2,1024]{1,0:T(2,128)S(1)}, f32[2,1024]{1,0:T(2,128)S(1)}, u32[]{:S(2)}, u32[]{:S(2)}) collective-permute-start(f32[2,1024]{1,0:T(2,128)S(1)} %get-tuple-element.74.shares_ref), channel_id=1, source_target_pairs={{2,0},{4,2},{6,4},{8,6},{10,8},{12,10},{14,12},{16,14},{18,16},{20... | collective-permute-start | bytes 24584 | tf_op jit(solution)/shard_map/ppermute | solution.py:278
  174.8 0.0 collective-permute-done.5
  174.8 0.6 broadcast_select_fusion
  175.5 0.0 copy-start.5
  175.5 0.4 slice.37
  175.9 3.8 %shard_map.92 = (bf16[1024,128]{1,0:T(8,128)(2,1)S(1)}, bf16[1024,128]{1,0:T(8,128)(2,1)S(1)}) custom-call(bf16[2048,128]{1,0:T(8,128)(2,1)S(1)} %bitcast.49, bf16[1024,128]{1,0:T(8,128)(2,1)S(1)} %bitcast.42, bf16[1024,128]{1,0:T(8,128)(2,1)S(1)} %bitcast.47, bf16[128,128]{1,0:T(8,128)(2,1)S(1)} %bitcast.52), custom_call_target="tpu_custom_call" | custom-call | tf_op jit(solution)/shard_map/pallas_call | solution.py:389
  179.7 0.0 collective-permute-done.4.shares_next_ref
  179.7 0.0 copy-done.7
  179.7 0.0 copy-done.9
  179.7 0.0 copy-done.5
  179.7 0.0 copy-start.11
  179.7 1.6 copy-done.11
  181.3 3.7 %shard_map.93 = (bf16[1024,128]{1,0:T(8,128)(2,1)}, bf16[1024,128]{1,0:T(8,128)(2,1)}) custom-call(bf16[1024,128]{1,0:T(8,128)(2,1)S(1)} %bitcast.30, bf16[1024,128]{1,0:T(8,128)(2,1)S(1)} %bitcast.37, bf16[2048,128]{1,0:T(8,128)(2,1)S(1)} %collective-permute-done.2.qg_ref.qg_next_ref, f32[2,1024]{1,0:T(2,128)S(1)} %get-tuple-element.74.shares_ref, ...), custom_call_target="tpu_custom_call" | custom-call | tf_op jit(solution)/shard_map/pallas_call | solution.py:398
  (7 shorter events, 0.1 us)
Async XLA Ops:
  0.6 12.6 %copy-start.3 = (bf16[1,1024,128]{2,1,0:T(8,128)(2,1)S(1)}, bf16[1,1024,128]{2,1,0:T(8,128)(2,1)}, u32[]{:S(2)}) copy-start(bf16[1,1024,128]{2,1,0:T(8,128)(2,1)} %param.9) | copy-start | bytes 786436
  0.6 12.6 %copy-start.2 = (bf16[1,1024,128]{2,1,0:T(8,128)(2,1)S(1)}, bf16[1,1024,128]{2,1,0:T(8,128)(2,1)}, u32[]{:S(2)}) copy-start(bf16[1,1024,128]{2,1,0:T(8,128)(2,1)} %param.8) | copy-start | bytes 786436
  0.7 12.6 %copy-start.1 = (bf16[1,1024,128]{2,1,0:T(8,128)(2,1)S(1)}, bf16[1,1024,128]{2,1,0:T(8,128)(2,1)}, u32[]{:S(2)}) copy-start(bf16[1,1024,128]{2,1,0:T(8,128)(2,1)} %param.10) | copy-start | bytes 786436
  0.7 12.6 %copy-start = (bf16[1,1024,128]{2,1,0:T(8,128)(2,1)S(1)}, bf16[1,1024,128]{2,1,0:T(8,128)(2,1)}, u32[]{:S(2)}) copy-start(bf16[1,1024,128]{2,1,0:T(8,128)(2,1)} %param.7) | copy-start | bytes 786436
  1.8 12.6 %collective-permute-start.1 = (bf16[2048,128]{1,0:T(8,128)(2,1)S(1)}, bf16[2048,128]{1,0:T(8,128)(2,1)S(1)}, u32[]{:S(2)}, u32[]{:S(2)}) collective-permute-start(bf16[2048,128]{1,0:T(8,128)(2,1)S(1)} %pad_maximum_fusion), channel_id=1, source_target_pairs={{0,2},{2,0},{4,6},{6,4},{8,10},{10,8},{12,14},{14,12},{16,18},{18,... | collective-permute-start | bytes 1572872 | tf_op jit(solution)/shard_map/ppermute | solution.py:282
  10.6 8.0 %collective-permute-start = (bf16[2048,128]{1,0:T(8,128)(2,1)S(1)}, bf16[2048,128]{1,0:T(8,128)(2,1)S(1)}, u32[]{:S(2)}, u32[]{:S(2)}) collective-permute-start(bf16[2048,128]{1,0:T(8,128)(2,1)S(1)} %pad_maximum_fusion), channel_id=1, source_target_pairs={{0,2},{2,4},{4,6},{6,8},{8,10},{10,12},{12,14},{14,16},{16,18},{18... | collective-permute-start | bytes 1572872 | tf_op jit(solution)/shard_map/ppermute | solution.py:278
  21.6 67.3 %all-to-all-start = ((bf16[128,17,2,128]{3,2,1,0:T(2,128)(2,1)}), bf16[128,17,2,128]{3,2,1,0:T(2,128)(2,1)S(1)}, u32[]{:S(2)}, u32[]{:S(2)}) async-start(bf16[128,17,2,128]{3,2,1,0:T(2,128)(2,1)} %broadcast_dynamic-update-slice_fusion), calls=%async_computation | async-start | bytes 2228224 | tf_op jit(solution)/shard_map/all_to_all | solution.py:287
  39.3 16.6 %collective-permute-start.2 = (bf16[2048,128]{1,0:T(8,128)(2,1)S(1)}, bf16[2048,128]{1,0:T(8,128)(2,1)S(1)}, u32[]{:S(2)}, u32[]{:S(2)}) collective-permute-start(bf16[2048,128]{1,0:T(8,128)(2,1)S(1)} %pad_maximum_fusion.1), channel_id=1, source_target_pairs={{2,0},{4,2},{6,4},{8,6},{10,8},{12,10},{14,12},{16,14},{18,16},{20... | collective-permute-start | bytes 1572872 | tf_op jit(solution)/shard_map/ppermute | solution.py:278
  44.6 11.4 %collective-permute-start.3 = (f32[2,1024]{1,0:T(2,128)S(1)}, f32[2,1024]{1,0:T(2,128)S(1)}, u32[]{:S(2)}, u32[]{:S(2)}) collective-permute-start(f32[2,1024]{1,0:T(2,128)S(1)} %get-tuple-element.52.stats_ref), channel_id=1, source_target_pairs={{2,0},{4,2},{6,4},{8,6},{10,8},{12,10},{14,12},{16,14},{18,16},{20... | collective-permute-start | bytes 24584 | tf_op jit(solution)/shard_map/ppermute | solution.py:278
  50.0 1.3 copy-start.4
  51.4 1.3 copy-start.6
  52.7 0.8 copy-start.12
  53.5 0.8 copy-start.14
  54.3 0.8 copy-start.16
  91.4 74.8 %all-to-all-start.1 = ((bf16[128,17,2,128]{3,2,1,0:T(2,128)(2,1)}), bf16[128,17,2,128]{3,2,1,0:T(2,128)(2,1)S(1)}, u32[]{:S(2)}, u32[]{:S(2)}) async-start(bf16[128,17,2,128]{3,2,1,0:T(2,128)(2,1)} %shard_map.88), calls=%async_computation.1 | async-start | bytes 2228224 | tf_op jit(solution)/shard_map/all_to_all | solution.py:287
  113.7 54.7 %copy-start.13 = (f32[128,1024]{1,0:T(8,128)S(1)}, f32[128,1024]{1,0:T(8,128)}, u32[]{:S(2)}) copy-start(f32[128,1024]{1,0:T(8,128)} %copy-done.12) | copy-start | bytes 1572868
  115.0 1.4 copy-start.8
  116.4 1.4 copy-start.10
  166.2 2.2 %copy-start.15 = (f32[128,1024]{1,0:T(8,128)S(1)}, f32[128,1024]{1,0:T(8,128)}, u32[]{:S(2)}) copy-start(f32[128,1024]{1,0:T(8,128)} %copy-done.14) | copy-start | bytes 1572868
  166.3 2.2 %copy-start.17 = (f32[128,1024]{1,0:T(8,128)S(1)}, f32[128,1024]{1,0:T(8,128)}, u32[]{:S(2)}) copy-start(f32[128,1024]{1,0:T(8,128)} %copy-done.16) | copy-start | bytes 1572868
  166.4 8.4 %collective-permute-start.5 = (bf16[128,9,2,128]{3,2,1,0:T(2,128)(2,1)S(1)}, bf16[128,9,2,128]{3,2,1,0:T(2,128)(2,1)S(1)}, u32[]{:S(2)}, u32[]{:S(2)}) collective-permute-start(bf16[128,9,2,128]{3,2,1,0:T(2,128)(2,1)S(1)} %get-tuple-element.79), channel_id=1, source_target_pairs={{0,2},{2,0},{4,6},{6,4},{8,10},{10,8},{12,14},{14,12},{16,18},{18,... | collective-permute-start | bytes 1769480 | tf_op jit(solution)/shard_map/ppermute | solution.py:282
  168.5 11.2 %copy-start.7 = (bf16[1024,1024]{1,0:T(8,128)(2,1)S(1)}, bf16[1024,1024]{1,0:T(8,128)(2,1)}, u32[]{:S(2)}) copy-start(bf16[1024,1024]{1,0:T(8,128)(2,1)} %copy-done.6) | copy-start | bytes 6291460
  168.5 11.2 %copy-start.9 = (bf16[1024,1024]{1,0:T(8,128)(2,1)S(1)}, bf16[1024,1024]{1,0:T(8,128)(2,1)}, u32[]{:S(2)}) copy-start(bf16[1024,1024]{1,0:T(8,128)(2,1)} %copy-done.8) | copy-start | bytes 6291460
  172.4 7.3 %collective-permute-start.4 = (f32[2,1024]{1,0:T(2,128)S(1)}, f32[2,1024]{1,0:T(2,128)S(1)}, u32[]{:S(2)}, u32[]{:S(2)}) collective-permute-start(f32[2,1024]{1,0:T(2,128)S(1)} %get-tuple-element.74.shares_ref), channel_id=1, source_target_pairs={{2,0},{4,2},{6,4},{8,6},{10,8},{12,10},{14,12},{16,14},{18,16},{20... | collective-permute-start | bytes 24584 | tf_op jit(solution)/shard_map/ppermute | solution.py:278
  175.5 4.2 %copy-start.5 = (bf16[1024,1024]{1,0:T(8,128)(2,1)S(1)}, bf16[1024,1024]{1,0:T(8,128)(2,1)}, u32[]{:S(2)}) copy-start(bf16[1024,1024]{1,0:T(8,128)(2,1)} %copy-done.4) | copy-start | bytes 6291460
  179.7 1.6 copy-start.11

commit v4 on v3

--- a/solution.py
+++ b/solution.py
@@ -201,7 +201,7 @@
         shares_ref[1:2, cols] = delta
 
 
-def partner_terms_kernel(scale, factor, qg_ref, k_ref, v_ref, notes_ref, dk_ref, dv_ref, s_ref, w_ref):
+def partner_terms_kernel(scale, factor, qg_ref, k_ref, v_ref, notes_ref, _, dk_ref, dv_ref, s_ref, w_ref):
     rows = k_ref.shape[0]
     q_ref, g_ref = qg_ref.at[:rows], qg_ref.at[rows:]
     elsewhere, pushed_there = read_notes(notes_ref, rows)
@@ -389,11 +389,11 @@
     dk, dv = pl.pallas_call(
         functools.partial(partner_terms_kernel, scale, factor),
         out_shape=(block, block),
-        in_specs=[vmem] * 4,
+        in_specs=[vmem] * 5,
         out_specs=(vmem,) * 2,
         scratch_shapes=[pltpu.VMEM((rows, rows), BF16)] * 2,
         compiler_params=params,
-    )(qg, k, v, notes)
+    )(qg, k, v, notes, wn)
     one, two = pltpu.VMEM((rows, width), BF16), pltpu.VMEM((rows, 2 * width), BF16)
     key_grad, value_grad = pl.pallas_call(
         functools.partial(sum_kernel, factor),

time: 189 us -> 190 us (level)
  the two profiles are of different devices: /device:TPU:1 before, /device:TPU:34 now
where the time goes in v4:
time: 190 us; the launch traced here: 189 us
  waiting for transfers between devices  103 us (54%)
  starting transfers between devices  48.3 us (25%)
  Pallas kernels  23.3 us (12%)
  local copies, waits for them, and re-layouts  10.5 us (6%)
    all_to_all x2, waiting for transfers between devices, exchange(): return lax.all_to_all(x, 'seq', 0, 0, axis_index_groups=groups, tiled=True)  59.5 us
    ppermute x4, waiting for transfers between devices, shifted(): lax.ppermute(x, 'seq', [(i, i + distance) for i in range(n) if 0 <= i + d...  44 us
    all_to_all x2, starting transfers between devices, exchange(): return lax.all_to_all(x, 'seq', 0, 0, axis_index_groups=groups, tiled=True)  24.6 us
    ppermute x4, starting transfers between devices, shifted(): lax.ppermute(x, 'seq', [(i, i + distance) for i in range(n) if 0 <= i + d...  14.6 us
    unnamed x40, local copies, waits for them, and re-layouts  9.41 us
    ppermute x2, starting transfers between devices, swapped(): lax.ppermute(x, 'seq', [(i, i ^ 1) for i in range(lax.axis_size('seq'))])  9.24 us
    pallas_call x1, Pallas kernels, local(): pl.pallas_call(functools.partial(query_kernel, scale, factor), out_shape=...  3.87 us
  transfers between devices with their start and end apart: 8, of which 4 were waited for; matrix products, arithmetic and copies ran while one was open for 1% of the time, Pallas kernels for 7%

profile of v4, /device:TPU:34, one launch (start us, length us, event | category | flops | bytes accessed | tf_op | source)
XLA Modules:
  0.0 189.1 jit_solution(6039302531900811172)
XLA Ops:
  0.6 0.0 copy-start.3
  0.6 0.0 copy-start.2
  0.7 0.0 copy-start.1
  0.7 0.0 copy-start
  0.7 1.1 pad_maximum_fusion
  1.8 1.9 %collective-permute-start.1 = (bf16[2048,128]{1,0:T(8,128)(2,1)S(1)}, bf16[2048,128]{1,0:T(8,128)(2,1)S(1)}, u32[]{:S(2)}, u32[]{:S(2)}) collective-permute-start(bf16[2048,128]{1,0:T(8,128)(2,1)S(1)} %pad_maximum_fusion), channel_id=1, source_target_pairs={{0,2},{2,0},{4,6},{6,4},{8,10},{10,8},{12,14},{14,12},{16,18},{18,... | collective-permute-start | bytes 1572872 | tf_op jit(solution)/shard_map/ppermute | solution.py:282
  3.7 2.4 %collective-permute-start = (bf16[2048,128]{1,0:T(8,128)(2,1)S(1)}, bf16[2048,128]{1,0:T(8,128)(2,1)S(1)}, u32[]{:S(2)}, u32[]{:S(2)}) collective-permute-start(bf16[2048,128]{1,0:T(8,128)(2,1)S(1)} %pad_maximum_fusion), channel_id=1, source_target_pairs={{0,2},{2,4},{4,6},{6,8},{8,10},{10,12},{12,14},{14,16},{16,18},{18... | collective-permute-start | bytes 1572872 | tf_op jit(solution)/shard_map/ppermute | solution.py:278
  6.8 0.0 copy-done.3
  6.8 0.0 copy-done.2
  6.8 0.0 copy-done.1
  6.8 0.0 copy-done
  6.9 1.2 shard_map.84.own_ref
  8.0 0.0 collective-permute-done.1
  8.0 10.7 %collective-permute-done.before_ref = bf16[2048,128]{1,0:T(8,128)(2,1)S(1)} collective-permute-done((bf16[2048,128]{1,0:T(8,128)(2,1)S(1)}, bf16[2048,128]{1,0:T(8,128)(2,1)S(1)}, u32[]{:S(2)}, u32[]{:S(2)}) %collective-permute-start) | collective-permute-done | bytes 524320 | tf_op jit(solution)/shard_map/ppermute | solution.py:278
  18.8 2.3 %shard_map.85 = (f32[2,1024]{1,0:T(2,128)S(1)}, bf16[128,128]{1,0:T(8,128)(2,1)S(1)}, bf16[128,17,2,128]{3,2,1,0:T(2,128)(2,1)}) custom-call(s32[1]{0:T(128)} %bitcast.2.at, s32[1]{0:T(128)} %bitcast.23.route, bf16[1024,128]{1,0:T(8,128)(2,1)S(1)} %bitcast.25, bf16[1024,128]{1,0:T(8,128)(2,1)S(1)} %bitcast.32, f32[3,1024]{1,0:T(4,128)S(1)} %shard_map.84.own_ref, ...), custom_call_target="tpu_custom_call" | custom-call | tf_op jit(solution)/shard_map/pallas_call | solution.py:326
  21.1 0.7 broadcast_dynamic-update-slice_fusion
  21.8 17.8 %all-to-all-start = ((bf16[128,17,2,128]{3,2,1,0:T(2,128)(2,1)}), bf16[128,17,2,128]{3,2,1,0:T(2,128)(2,1)S(1)}, u32[]{:S(2)}, u32[]{:S(2)}) async-start(bf16[128,17,2,128]{3,2,1,0:T(2,128)(2,1)} %broadcast_dynamic-update-slice_fusion), calls=%async_computation | async-start | bytes 2228224 | tf_op jit(solution)/shard_map/all_to_all | solution.py:287
  39.6 4.3 %collective-permute-start.2 = (bf16[2048,128]{1,0:T(8,128)(2,1)S(1)}, bf16[2048,128]{1,0:T(8,128)(2,1)S(1)}, u32[]{:S(2)}, u32[]{:S(2)}) collective-permute-start(bf16[2048,128]{1,0:T(8,128)(2,1)S(1)} %pad_maximum_fusion.1), channel_id=1, source_target_pairs={{2,0},{4,2},{6,4},{8,6},{10,8},{12,10},{14,12},{16,14},{18,16},{20... | collective-permute-start | bytes 1572872 | tf_op jit(solution)/shard_map/ppermute | solution.py:278
  43.8 4.8 %collective-permute-start.3 = (f32[2,1024]{1,0:T(2,128)S(1)}, f32[2,1024]{1,0:T(2,128)S(1)}, u32[]{:S(2)}, u32[]{:S(2)}) collective-permute-start(f32[2,1024]{1,0:T(2,128)S(1)} %get-tuple-element.52.stats_ref), channel_id=1, source_target_pairs={{2,0},{4,2},{6,4},{8,6},{10,8},{12,10},{14,12},{16,14},{18,16},{20... | collective-permute-start | bytes 24584 | tf_op jit(solution)/shard_map/ppermute | solution.py:278
  48.6 3.5 %shard_map.86 = (f32[128,1024]{1,0:T(8,128)S(1)}, f32[128,1024]{1,0:T(8,128)S(1)}, f32[128,1024]{1,0:T(8,128)S(1)}, bf16[1024,1024]{1,0:T(8,128)(2,1)S(1)}, bf16...) custom-call(s32[1]{0:T(128)} %bitcast.2.at, bf16[1024,128]{1,0:T(8,128)(2,1)S(1)} %bitcast.28, ...), custom_call_target="tpu_custom_call" | custom-call | tf_op jit(solution)/shard_map/pallas_call | solution.py:342
  52.0 0.0 copy-start.4
  52.1 1.3 copy-done.4
  53.4 0.0 copy-start.6
  53.4 1.3 copy-done.6
  54.7 0.0 copy-start.13
  54.7 0.8 copy-done.13
  55.5 0.0 copy-start.15
  55.5 0.8 copy-done.15
  56.3 0.0 copy-start.17
  56.3 0.8 copy-done.17
  57.1 33.3 %collective-permute-done.2.qg_ref.qg_next_ref = bf16[2048,128]{1,0:T(8,128)(2,1)S(1)} collective-permute-done((bf16[2048,128]{1,0:T(8,128)(2,1)S(1)}, bf16[2048,128]{1,0:T(8,128)(2,1)S(1)}, u32[]{:S(2)}, u32[]{:S(2)}) %collective-permute-start.2) | collective-permute-done | bytes 524320 | tf_op jit(solution)/shard_map/ppermute | solution.py:278
  90.4 0.8 copy-done.10
  91.2 0.0 collective-permute-done.3.stats_ref
  91.2 7.2 %all-to-all-done.x_ref = bf16[128,17,2,128]{3,2,1,0:T(2,128)(2,1)S(1)} async-done(((bf16[128,17,2,128]{3,2,1,0:T(2,128)(2,1)}), bf16[128,17,2,128]{3,2,1,0:T(2,128)(2,1)S(1)}, u32[]{:S(2)}, u32[]{:S(2)}) %all-to-all-start) | async-done | bytes 1114144 | tf_op jit(solution)/shard_map/all_to_all | solution.py:287
  98.5 0.5 shard_map.87
  99.0 2.0 %shard_map.88 = bf16[128,17,2,128]{3,2,1,0:T(2,128)(2,1)} custom-call(s32[1,128]{1,0:T(1,128)S(1)} %get-tuple-element.60.partner_ref, s32[1,128]{1,0:T(1,128)S(1)} %get-tuple-element.61.inverse_ref, bf16[128,17,2,128]{3,2,1,0:T(2,128)(2,1)S(1)} %all-to-all-done.x_ref), custom_call_target="tpu_custom_call" | custom-call | tf_op jit(solution)/shard_map/pallas_call | solution.py:354
  101.0 6.8 %all-to-all-start.1 = ((bf16[128,17,2,128]{3,2,1,0:T(2,128)(2,1)}), bf16[128,17,2,128]{3,2,1,0:T(2,128)(2,1)}, u32[]{:S(2)}, u32[]{:S(2)}) async-start(bf16[128,17,2,128]{3,2,1,0:T(2,128)(2,1)} %shard_map.88), calls=%async_computation.1 | async-start | bytes 2228224 | tf_op jit(solution)/shard_map/all_to_all | solution.py:287
  107.8 0.0 copy-start.11
  107.8 1.0 copy-done.11
  108.8 1.3 shard_map.89
  110.1 0.0 copy-start.8
  110.1 1.4 copy-done.8
  111.5 52.3 %all-to-all-done.1.x_ref = bf16[128,17,2,128]{3,2,1,0:T(2,128)(2,1)} async-done(((bf16[128,17,2,128]{3,2,1,0:T(2,128)(2,1)}), bf16[128,17,2,128]{3,2,1,0:T(2,128)(2,1)}, u32[]{:S(2)}, u32[]{:S(2)}) %all-to-all-start.1) | async-done | bytes 1114144 | tf_op jit(solution)/shard_map/all_to_all | solution.py:287
  163.8 1.3 shard_map.90
  165.1 7.3 %collective-permute-start.5 = (bf16[128,9,2,128]{3,2,1,0:T(2,128)(2,1)S(1)}, bf16[128,9,2,128]{3,2,1,0:T(2,128)(2,1)S(1)}, u32[]{:S(2)}, u32[]{:S(2)}) collective-permute-start(bf16[128,9,2,128]{3,2,1,0:T(2,128)(2,1)S(1)} %get-tuple-element.79), channel_id=1, source_target_pairs={{0,2},{2,0},{4,6},{6,4},{8,10},{10,8},{12,14},{14,12},{16,18},{18,... | collective-permute-start | bytes 1769480 | tf_op jit(solution)/shard_map/ppermute | solution.py:282
  172.5 0.0 copy-done.14
  172.5 0.0 copy-done.16
  172.5 0.0 copy-start.18
  172.5 1.0 copy-done.18
  173.5 3.9 %shard_map.91 = (bf16[1024,128]{1,0:T(8,128)(2,1)}, bf16[1024,128]{1,0:T(8,128)(2,1)}, f32[2,1024]{1,0:T(2,128)S(1)}) custom-call(bf16[1024,128]{1,0:T(8,128)(2,1)S(1)} %bitcast.29, bf16[1024,128]{1,0:T(8,128)(2,1)S(1)} %bitcast.36, bf16[2048,128]{1,0:T(8,128)(2,1)S(1)} %bitcast.51, f32[2,1024]{1,0:T(2,128)S(1)} %get-tuple-element.52.stats_ref, ...), custom_call_target="tpu_custom_call" | custom-call | tf_op jit(solution)/shard_map/pallas_call | solution.py:381
  177.4 3.1 %collective-permute-start.4 = (f32[2,1024]{1,0:T(2,128)S(1)}, f32[2,1024]{1,0:T(2,128)S(1)}, u32[]{:S(2)}, u32[]{:S(2)}) collective-permute-start(f32[2,1024]{1,0:T(2,128)S(1)} %get-tuple-element.74.shares_ref), channel_id=1, source_target_pairs={{2,0},{4,2},{6,4},{8,6},{10,8},{12,10},{14,12},{16,14},{18,16},{20... | collective-permute-start | bytes 24584 | tf_op jit(solution)/shard_map/ppermute | solution.py:278
  180.5 0.0 collective-permute-done.5
  180.6 0.0 copy-start.12
  180.6 0.6 broadcast_select_fusion
  181.2 0.0 copy-start.7
  181.3 0.4 slice.37
  181.6 0.0 copy-start.5
  181.7 3.8 %shard_map.92 = (bf16[1024,128]{1,0:T(8,128)(2,1)S(1)}, bf16[1024,128]{1,0:T(8,128)(2,1)S(1)}) custom-call(bf16[2048,128]{1,0:T(8,128)(2,1)S(1)} %bitcast.49, bf16[1024,128]{1,0:T(8,128)(2,1)S(1)} %bitcast.42, bf16[1024,128]{1,0:T(8,128)(2,1)S(1)} %bitcast.47, bf16[128,128]{1,0:T(8,128)(2,1)S(1)} %bitcast.52, bf16[1024,1024]{1,0:T(8,128)(2,1)S(1)} %get-tuple-element.78._.wn_ref), custom_call_target="tpu_custom_call" | custom-call | tf_op jit(solution)/shard_map/pallas_call | solution.py:389
  185.4 0.0 collective-permute-done.4.shares_next_ref
  185.4 0.0 copy-done.9
  185.4 0.0 copy-done.12
  185.5 0.0 copy-done.7
  185.5 0.0 copy-done.5
  185.5 3.6 %shard_map.93 = (bf16[1024,128]{1,0:T(8,128)(2,1)}, bf16[1024,128]{1,0:T(8,128)(2,1)}) custom-call(bf16[1024,128]{1,0:T(8,128)(2,1)S(1)} %bitcast.30, bf16[1024,128]{1,0:T(8,128)(2,1)S(1)} %bitcast.37, bf16[2048,128]{1,0:T(8,128)(2,1)S(1)} %copy-done.12, f32[2,1024]{1,0:T(2,128)S(1)} %get-tuple-element.74.shares_ref, ...), custom_call_target="tpu_custom_call" | custom-call | tf_op jit(solution)/shard_map/pallas_call | solution.py:398
  (9 shorter events, 0.2 us)
Async XLA Ops:
  0.6 6.2 %copy-start.3 = (bf16[1,1024,128]{2,1,0:T(8,128)(2,1)S(1)}, bf16[1,1024,128]{2,1,0:T(8,128)(2,1)}, u32[]{:S(2)}) copy-start(bf16[1,1024,128]{2,1,0:T(8,128)(2,1)} %param.9) | copy-start | bytes 786436
  0.6 6.2 %copy-start.2 = (bf16[1,1024,128]{2,1,0:T(8,128)(2,1)S(1)}, bf16[1,1024,128]{2,1,0:T(8,128)(2,1)}, u32[]{:S(2)}) copy-start(bf16[1,1024,128]{2,1,0:T(8,128)(2,1)} %param.8) | copy-start | bytes 786436
  0.7 6.2 %copy-start.1 = (bf16[1,1024,128]{2,1,0:T(8,128)(2,1)S(1)}, bf16[1,1024,128]{2,1,0:T(8,128)(2,1)}, u32[]{:S(2)}) copy-start(bf16[1,1024,128]{2,1,0:T(8,128)(2,1)} %param.10) | copy-start | bytes 786436
  0.7 6.2 %copy-start = (bf16[1,1024,128]{2,1,0:T(8,128)(2,1)S(1)}, bf16[1,1024,128]{2,1,0:T(8,128)(2,1)}, u32[]{:S(2)}) copy-start(bf16[1,1024,128]{2,1,0:T(8,128)(2,1)} %param.7) | copy-start | bytes 786436
  1.8 6.2 %collective-permute-start.1 = (bf16[2048,128]{1,0:T(8,128)(2,1)S(1)}, bf16[2048,128]{1,0:T(8,128)(2,1)S(1)}, u32[]{:S(2)}, u32[]{:S(2)}) collective-permute-start(bf16[2048,128]{1,0:T(8,128)(2,1)S(1)} %pad_maximum_fusion), channel_id=1, source_target_pairs={{0,2},{2,0},{4,6},{6,4},{8,10},{10,8},{12,14},{14,12},{16,18},{18,... | collective-permute-start | bytes 1572872 | tf_op jit(solution)/shard_map/ppermute | solution.py:282
  3.7 15.0 %collective-permute-start = (bf16[2048,128]{1,0:T(8,128)(2,1)S(1)}, bf16[2048,128]{1,0:T(8,128)(2,1)S(1)}, u32[]{:S(2)}, u32[]{:S(2)}) collective-permute-start(bf16[2048,128]{1,0:T(8,128)(2,1)S(1)} %pad_maximum_fusion), channel_id=1, source_target_pairs={{0,2},{2,4},{4,6},{6,8},{8,10},{10,12},{12,14},{14,16},{16,18},{18... | collective-permute-start | bytes 1572872 | tf_op jit(solution)/shard_map/ppermute | solution.py:278
  21.8 76.6 %all-to-all-start = ((bf16[128,17,2,128]{3,2,1,0:T(2,128)(2,1)}), bf16[128,17,2,128]{3,2,1,0:T(2,128)(2,1)S(1)}, u32[]{:S(2)}, u32[]{:S(2)}) async-start(bf16[128,17,2,128]{3,2,1,0:T(2,128)(2,1)} %broadcast_dynamic-update-slice_fusion), calls=%async_computation | async-start | bytes 2228224 | tf_op jit(solution)/shard_map/all_to_all | solution.py:287
  39.6 50.8 %collective-permute-start.2 = (bf16[2048,128]{1,0:T(8,128)(2,1)S(1)}, bf16[2048,128]{1,0:T(8,128)(2,1)S(1)}, u32[]{:S(2)}, u32[]{:S(2)}) collective-permute-start(bf16[2048,128]{1,0:T(8,128)(2,1)S(1)} %pad_maximum_fusion.1), channel_id=1, source_target_pairs={{2,0},{4,2},{6,4},{8,6},{10,8},{12,10},{14,12},{16,14},{18,16},{20... | collective-permute-start | bytes 1572872 | tf_op jit(solution)/shard_map/ppermute | solution.py:278
  43.8 47.4 %collective-permute-start.3 = (f32[2,1024]{1,0:T(2,128)S(1)}, f32[2,1024]{1,0:T(2,128)S(1)}, u32[]{:S(2)}, u32[]{:S(2)}) collective-permute-start(f32[2,1024]{1,0:T(2,128)S(1)} %get-tuple-element.52.stats_ref), channel_id=1, source_target_pairs={{2,0},{4,2},{6,4},{8,6},{10,8},{12,10},{14,12},{16,14},{18,16},{20... | collective-permute-start | bytes 24584 | tf_op jit(solution)/shard_map/ppermute | solution.py:278
  52.0 1.3 copy-start.4
  53.4 1.3 copy-start.6
  54.7 0.8 copy-start.13
  55.5 0.8 copy-start.15
  56.3 0.8 copy-start.17
  90.4 0.8 copy-start.10
  101.0 62.8 %all-to-all-start.1 = ((bf16[128,17,2,128]{3,2,1,0:T(2,128)(2,1)}), bf16[128,17,2,128]{3,2,1,0:T(2,128)(2,1)}, u32[]{:S(2)}, u32[]{:S(2)}) async-start(bf16[128,17,2,128]{3,2,1,0:T(2,128)(2,1)} %shard_map.88), calls=%async_computation.1 | async-start | bytes 2228224 | tf_op jit(solution)/shard_map/all_to_all | solution.py:287
  107.8 1.0 copy-start.11
  110.1 1.4 copy-start.8
  163.8 8.7 %copy-start.14 = (f32[128,1024]{1,0:T(8,128)S(1)}, f32[128,1024]{1,0:T(8,128)}, u32[]{:S(2)}) copy-start(f32[128,1024]{1,0:T(8,128)} %copy-done.13) | copy-start | bytes 1572868
  163.8 8.7 %copy-start.16 = (f32[128,1024]{1,0:T(8,128)S(1)}, f32[128,1024]{1,0:T(8,128)}, u32[]{:S(2)}) copy-start(f32[128,1024]{1,0:T(8,128)} %copy-done.15) | copy-start | bytes 1572868
  165.1 15.4 %collective-permute-start.5 = (bf16[128,9,2,128]{3,2,1,0:T(2,128)(2,1)S(1)}, bf16[128,9,2,128]{3,2,1,0:T(2,128)(2,1)S(1)}, u32[]{:S(2)}, u32[]{:S(2)}) collective-permute-start(bf16[128,9,2,128]{3,2,1,0:T(2,128)(2,1)S(1)} %get-tuple-element.79), channel_id=1, source_target_pairs={{0,2},{2,0},{4,6},{6,4},{8,10},{10,8},{12,14},{14,12},{16,18},{18,... | collective-permute-start | bytes 1769480 | tf_op jit(solution)/shard_map/ppermute | solution.py:282
  172.5 1.0 copy-start.18
  173.5 11.9 %copy-start.9 = (bf16[1024,1024]{1,0:T(8,128)(2,1)S(1)}, bf16[1024,1024]{1,0:T(8,128)(2,1)}, u32[]{:S(2)}) copy-start(bf16[1024,1024]{1,0:T(8,128)(2,1)} %copy-done.8) | copy-start | bytes 6291460
  177.4 8.0 %collective-permute-start.4 = (f32[2,1024]{1,0:T(2,128)S(1)}, f32[2,1024]{1,0:T(2,128)S(1)}, u32[]{:S(2)}, u32[]{:S(2)}) collective-permute-start(f32[2,1024]{1,0:T(2,128)S(1)} %get-tuple-element.74.shares_ref), channel_id=1, source_target_pairs={{2,0},{4,2},{6,4},{8,6},{10,8},{12,10},{14,12},{16,14},{18,16},{20... | collective-permute-start | bytes 24584 | tf_op jit(solution)/shard_map/ppermute | solution.py:278
  180.6 4.9 %copy-start.12 = (bf16[2048,128]{1,0:T(8,128)(2,1)S(1)}, bf16[2048,128]{1,0:T(8,128)(2,1)}, u32[]{:S(2)}) copy-start(bf16[2048,128]{1,0:T(8,128)(2,1)} %copy-done.10) | copy-start | bytes 1572868
  181.2 4.2 %copy-start.7 = (bf16[1024,1024]{1,0:T(8,128)(2,1)S(1)}, bf16[1024,1024]{1,0:T(8,128)(2,1)}, u32[]{:S(2)}) copy-start(bf16[1024,1024]{1,0:T(8,128)(2,1)} %copy-done.6) | copy-start | bytes 6291460
  181.6 3.8 %copy-start.5 = (bf16[1024,1024]{1,0:T(8,128)(2,1)S(1)}, bf16[1024,1024]{1,0:T(8,128)(2,1)}, u32[]{:S(2)}) copy-start(bf16[1024,1024]{1,0:T(8,128)(2,1)} %copy-done.4) | copy-start | bytes 6291460
